TPU v7x, 512 devices: a whole 4x8x8 slice. The times are simulated.
512 devices in a mesh: member: 4 (over y_lo), space: 128 (over z, y_hi, x, core).
Axes of the slice: x: 4, y: 8 (y_hi: 2, y_lo: 4; y = y_hi * 4 + y_lo), z: 8, core: 2. Of those that a mesh axis runs over, the one named last changes fastest.
Arguments:
- ensemble_prediction: bfloat16 [4, 300, 2048, 128], P('member', None, 'space'), may hold values from -6 to 6
- observed_analysis: bfloat16 [300, 2048, 128], P(None, 'space'), may hold values from -6 to 6
- validity_flags: int32 [2, 2048, 128], P(None, 'space'), may hold values from 0 to 1, as said below
Outputs:
- point_score: float32 [300, 2048, 128], P(None, 'space')
- channel_loss: float32 [300], replicated
Inputs may be any that keep to these rules, and one draw needn't show every extreme that they name: `validity_flags`: 0 or 1 for each point and group; every point of latitude row 180 is valid in both groups.
All inputs are finite; a program needn't handle non-finite values.
Results may differ from a plain program's by a relative error of at most 0.0003.
Values may be sent and summed in bfloat16 or wider, within the bound.
No kernel may reach another device: no remote copies, remote signals or barrier semaphores. Data moves between devices by JAX's collectives and lax.ppermute only.
A program may use at most 64 MiB of HBM per device.

v0:
```python
import functools

import jax
import jax.numpy as jnp
from jax import lax
from jax.sharding import Mesh
from jax.sharding import PartitionSpec as P

VARIABLE_NUMBER = 300
ATMOS = 180
TILE_SITES = 128
LON = 720
ROWS = 360
SPACE = ("space_0", "space_1", "space_2", "space_3")


def sent_to_all(x, axis):
    copies = jnp.broadcast_to(x, (lax.axis_size(axis), *x.shape))
    return lax.all_to_all(copies, axis, split_axis=0, concat_axis=0, tiled=True)


def laid_out(blocks, dim):
    blocks = jnp.moveaxis(blocks, 0, dim)
    dims = blocks.shape
    return blocks.reshape(*dims[:dim], dims[dim] * dims[dim + 1], *dims[dim + 2 :])


def collect(x, axis, dim):
    blocks = sent_to_all(x, axis)
    return laid_out(blocks, dim)


def by_axis(x, axes):
    return functools.reduce(lax.psum, axes, x)


def per_channel(values):
    is_ocean = jnp.arange(VARIABLE_NUMBER, dtype=jnp.int32) >= ATMOS
    return jnp.where(is_ocean, values[1], values[0])


def shards(ensemble_prediction, observed_analysis, validity_flags):
    blocks_here = observed_analysis.shape[1]
    realization_entries = lax.axis_size("member")
    lat_rows = min(ROWS, blocks_here * lax.axis_size(SPACE) * TILE_SITES // LON)
    first_point = lax.axis_index(SPACE) * (blocks_here * TILE_SITES)
    position = first_point + jnp.arange(blocks_here * TILE_SITES, dtype=jnp.int32).reshape(
        blocks_here, TILE_SITES
    )
    inside = (position < lat_rows * LON).astype(jnp.float32)
    lat_row = (position // LON).astype(jnp.float32)
    cosine = jnp.cos(jnp.pi * ((lat_row + 0.5) / lat_rows - 0.5))
    valid = inside[None] * (validity_flags > 0).astype(jnp.float32)
    weight = cosine[None] * valid
    local_area = jnp.sum(weight, axis=(1, 2))
    local_count = jnp.sum(valid, axis=(1, 2))
    is_ocean = jnp.arange(VARIABLE_NUMBER, dtype=jnp.int32) >= ATMOS
    weight_chan = jnp.where(is_ocean[:, None, None], weight[1][None], weight[0][None])
    coeff = (1.0 - 0.05 / realization_entries) / (
        2.0 * realization_entries * (realization_entries - 1)
    )
    gathered = lax.all_to_all(
        ensemble_prediction, "member", split_axis=2, concat_axis=0, tiled=True
    )
    share = blocks_here // realization_entries
    first_block = lax.axis_index("member") * share
    target_part = lax.dynamic_slice_in_dim(observed_analysis, first_block, share, 1).astype(
        jnp.float32
    )
    accuracy_component = jnp.zeros(target_part.shape, jnp.float32)
    dispersion_component = jnp.zeros(target_part.shape, jnp.float32)
    for leading_realization in range(realization_entries):
        lead = gathered[leading_realization].astype(jnp.float32)
        accuracy_component = accuracy_component + jnp.abs(lead - target_part)
        for trailing_realization in range(leading_realization + 1, realization_entries):
            dispersion_component = dispersion_component + jnp.abs(
                lead - gathered[trailing_realization].astype(jnp.float32)
            )
    partial_crps = accuracy_component / realization_entries - coeff * (2.0 * dispersion_component)
    crps = collect(partial_crps, "member", 1)
    area_sum, count = (by_axis(local_area, SPACE), by_axis(local_count, SPACE))
    scale_chan = per_channel(count / area_sum)
    point_score = crps * weight_chan * scale_chan[:, None, None]
    score_sums = by_axis(jnp.sum(point_score, axis=(1, 2)), SPACE)
    channel_loss = score_sums / per_channel(count)
    return (point_score, channel_loss)


def solution(mesh):
    split = Mesh(
        mesh.devices.reshape(mesh.shape["member"], 8, 2, 4, 2),
        ("member", "space_0", "space_1", "space_2", "space_3"),
    )
    return jax.shard_map(
        shards,
        mesh=split,
        in_specs=(P("member", None, SPACE, None), P(None, SPACE, None), P(None, SPACE, None)),
        out_specs=(P(None, SPACE, None), P()),
        check_vma=False,
    )
```

profile of v0, /device:TPU:1, one launch (start us, length us, event | category | flops | bytes accessed | tf_op | source)
XLA Modules:
  0.0 161.3 jit_solution(6692892398897394155)
XLA Ops:
  0.6 0.0 copy-start
  0.6 2.7 %copy.17 = bf16[1,300,16,128]{3,1,0,2:T(8,128)(2,1)} copy(bf16[1,300,16,128]{3,2,1,0:T(8,128)(2,1)} %param.3) | data formatting | bytes 2457600 | tf_op args[0]
  3.4 5.4 %all-to-all-start = ((bf16[1,300,16,128]{3,1,0,2:T(8,128)(2,1)}), bf16[1,300,16,128]{3,1,0,2:T(8,128)(2,1)S(1)}, u32[]{:S(2)}, u32[]{:S(2)}) async-start(bf16[1,300,16,128]{3,1,0,2:T(8,128)(2,1)} %copy.17), calls=%async_computation | async-start | bytes 2490368 | tf_op jit(solution)/shard_map/all_to_all | solution.py:62
  8.8 0.0 copy-done
  8.8 0.2 constant_dynamic-slice_fusion
  9.0 28.2 %all-to-all-done = bf16[1,300,16,128]{3,1,0,2:T(8,128)(2,1)S(1)} async-done(((bf16[1,300,16,128]{3,1,0,2:T(8,128)(2,1)}), bf16[1,300,16,128]{3,1,0,2:T(8,128)(2,1)S(1)}, u32[]{:S(2)}, u32[]{:S(2)}) %all-to-all-start) | async-done | bytes 1228832 | tf_op jit(solution)/shard_map/all_to_all | solution.py:62
  37.1 0.7 fusion.6
  37.9 0.2 copy.22
  38.1 1.8 %broadcast_in_dim.59 = f32[4,300,4,128]{3,2,1,0:T(4,128)} broadcast(f32[300,4,128]{2,1,0:T(4,128)S(1)} %copy.22), dimensions={1,2,3} | broadcast | bytes 3072000 | tf_op jit(solution)/shard_map/broadcast_in_dim | solution.py:18
  39.9 0.0 copy-start.1
  39.9 4.6 %all-to-all-start.1 = ((f32[4,300,4,128]{3,2,1,0:T(4,128)}), f32[4,300,4,128]{3,2,1,0:T(4,128)}, u32[]{:S(2)}, u32[]{:S(2)}) async-start(f32[4,300,4,128]{3,2,1,0:T(4,128)} %broadcast_in_dim.59), calls=%async_computation.1 | async-start | bytes 4915200 | tf_op jit(solution)/shard_map/all_to_all | solution.py:19
  44.6 0.1 fusion.27
  44.6 0.0 copy-done.1
  44.6 0.1 fusion.31
  44.7 0.1 select_reduce_fusion
  44.8 21.3 %all-reduce = (f32[2]{0:T(128)S(1)}, f32[2]{0:T(128)S(1)}) all-reduce(f32[2]{0:T(128)S(1)} %select_reduce_fusion, f32[2]{0:T(128)S(1)} %get-tuple-element.12), channel_id=1, replica_groups=mesh['member'=4,'space_0'=8,'space_1'=2,'space_2'=4,'space_3'=2] {'space..., use_global_device_ids=true, to_apply=%region_1.2 | all-reduce | flops 4 | bytes 32 | tf_op jit(solution)/shard_map/psum | solution.py:34
  66.2 23.2 %all-reduce.3 = (f32[2]{0:T(128)S(1)}, f32[2]{0:T(128)S(1)}) all-reduce(f32[2]{0:T(128)S(1)} %get-tuple-element.4, f32[2]{0:T(128)S(1)} %get-tuple-element.5), channel_id=1, replica_groups=mesh['member'=4,'space_0'=8,'space_1'=2,'space_2'=4,'space_3'=2] {'space..., use_global_device_ids=true, to_apply=%region_2.3 | all-reduce | flops 4 | bytes 32 | tf_op jit(solution)/shard_map/psum | solution.py:34
  89.4 8.9 %all-reduce.1 = (f32[2]{0:T(128)S(1)}, f32[2]{0:T(128)S(1)}) all-reduce(f32[2]{0:T(128)S(1)} %get-tuple-element.10, f32[2]{0:T(128)S(1)} %get-tuple-element.11), channel_id=1, replica_groups=mesh['member'=4,'space_0'=8,'space_1'=2,'space_2'=4,'space_3'=2] {'space..., use_global_device_ids=true, to_apply=%region_3.4 | all-reduce | flops 4 | bytes 32 | tf_op jit(solution)/shard_map/psum | solution.py:34
  98.3 6.0 %all-reduce.2 = (f32[2]{0:T(128)S(1)}, f32[2]{0:T(128)S(1)}) all-reduce(f32[2]{0:T(128)S(1)} %get-tuple-element.6, f32[2]{0:T(128)S(1)} %get-tuple-element.7), channel_id=1, replica_groups=mesh['member'=4,'space_0'=8,'space_1'=2,'space_2'=4,'space_3'=2] {'space..., use_global_device_ids=true, to_apply=%region_4.5 | all-reduce | flops 4 | bytes 32 | tf_op jit(solution)/shard_map/psum | solution.py:34
  104.3 0.6 fusion.34
  104.9 1.3 broadcast_select_fusion
  106.2 0.6 fusion.33
  106.8 0.0 all-to-all-done.1
  106.8 6.0 %multiply_reduce_fusion = f32[300]{0:T(512)S(1)} fusion(f32[300]{0:T(512)S(1)} %broadcast_select_fusion, f32[4,4,128]{2,1,0:T(4,128)S(1)} %bitcast.44, f32[4,4,128]{2,1,0:T(4,128)S(1)} %bitcast.43, pred[300]{0:T(512)(128)(4,1)S(1)} %iota_compare_fusion, f32[4,300,4,128]{3,2,1,0:T(4,128)} %all-to-all-done.1), kind=kLoop, calls=%fused_computation.2 | loop fusion | flops 2457300 | bytes 2476684 | tf_op jit(solution)/shard_map/reduce_sum | solution.py:84
  112.8 19.4 %psum.92 = f32[300]{0:T(512)S(1)} all-reduce(f32[300]{0:T(512)S(1)} %multiply_reduce_fusion), channel_id=1, replica_groups=mesh['member'=4,'space_0'=8,'space_1'=2,'space_2'=4,'space_3'=2] {'space..., use_global_device_ids=true, to_apply=%region_11.12 | all-reduce | flops 300 | bytes 2400 | tf_op jit(solution)/shard_map/psum | solution.py:34
  132.3 7.7 %psum.93 = f32[300]{0:T(512)S(1)} all-reduce(f32[300]{0:T(512)S(1)} %psum.92), channel_id=1, replica_groups=mesh['member'=4,'space_0'=8,'space_1'=2,'space_2'=4,'space_3'=2] {'space..., use_global_device_ids=true, to_apply=%region_12.13 | all-reduce | flops 300 | bytes 2400 | tf_op jit(solution)/shard_map/psum | solution.py:34
  139.9 6.0 %psum.94 = f32[300]{0:T(512)S(1)} all-reduce(f32[300]{0:T(512)S(1)} %psum.93), channel_id=1, replica_groups=mesh['member'=4,'space_0'=8,'space_1'=2,'space_2'=4,'space_3'=2] {'space..., use_global_device_ids=true, to_apply=%region_13.14 | all-reduce | flops 300 | bytes 2400 | tf_op jit(solution)/shard_map/psum | solution.py:34
  145.9 9.1 %psum.95 = f32[300]{0:T(512)S(1)} all-reduce(f32[300]{0:T(512)S(1)} %psum.94), channel_id=1, replica_groups=mesh['member'=4,'space_0'=8,'space_1'=2,'space_2'=4,'space_3'=2] {'space..., use_global_device_ids=true, to_apply=%region_14.15 | all-reduce | flops 300 | bytes 2400 | tf_op jit(solution)/shard_map/psum | solution.py:34
  155.0 1.9 %copy.23 = f32[300,4,4,128]{3,0,2,1:T(8,128)S(1)} copy(f32[300,4,4,128]{3,2,0,1:T(4,128)} %bitcast.13) | data formatting | bytes 4915200 | tf_op jit(solution)/shard_map/transpose | solution.py:23
  156.9 0.4 fusion
  157.3 2.2 %copy.24 = f32[300,16,128]{2,1,0:T(8,128)} copy(f32[300,16,128]{2,0,1:T(8,128)S(1)} %fusion) | data formatting | bytes 4915200
  159.5 1.8 %select_divide_fusion = f32[300]{0:T(512)} fusion(f32[300]{0:T(512)S(1)} %psum.95, f32[]{:T(128)} %bitcast.22, f32[]{:T(128)} %bitcast.21), kind=kLoop, calls=%fused_computation.54 | loop fusion | flops 900 | bytes 2408 | tf_op jit(solution)/shard_map/div | solution.py:85
  (4 shorter events, 0.0 us)
Async XLA Ops:
  0.6 8.2 %copy-start = (bf16[300,16,128]{2,1,0:T(8,128)(2,1)S(1)}, bf16[300,16,128]{2,1,0:T(8,128)(2,1)}, u32[]{:S(2)}) copy-start(bf16[300,16,128]{2,1,0:T(8,128)(2,1)} %param.4) | copy-start | bytes 3686404
  3.4 33.8 %all-to-all-start = ((bf16[1,300,16,128]{3,1,0,2:T(8,128)(2,1)}), bf16[1,300,16,128]{3,1,0,2:T(8,128)(2,1)S(1)}, u32[]{:S(2)}, u32[]{:S(2)}) async-start(bf16[1,300,16,128]{3,1,0,2:T(8,128)(2,1)} %copy.17), calls=%async_computation | async-start | bytes 2490368 | tf_op jit(solution)/shard_map/all_to_all | solution.py:62
  39.9 4.8 %copy-start.1 = (s32[2,16,128]{2,1,0:T(8,128)S(1)}, s32[2,16,128]{2,1,0:T(8,128)}, u32[]{:S(2)}) copy-start(s32[2,16,128]{2,1,0:T(8,128)} %param.5) | copy-start | bytes 49156
  39.9 66.9 %all-to-all-start.1 = ((f32[4,300,4,128]{3,2,1,0:T(4,128)}), f32[4,300,4,128]{3,2,1,0:T(4,128)}, u32[]{:S(2)}, u32[]{:S(2)}) async-start(f32[4,300,4,128]{3,2,1,0:T(4,128)} %broadcast_in_dim.59), calls=%async_computation.1 | async-start | bytes 4915200 | tf_op jit(solution)/shard_map/all_to_all | solution.py:19
where the time goes:
time: 162 us; the launch traced here: 161 us
  blocking collectives  102 us (63%)
  waiting for transfers between devices  28.2 us (17%)
  other arithmetic  10.5 us (6%)
  local copies, waits for them, and re-layouts  10.2 us (6%)
  starting transfers between devices  10.1 us (6%)
    psum x8, blocking collectives, by_axis(): return functools.reduce(lax.psum, axes, x)  102 us
    all_to_all x1, waiting for transfers between devices, shards(): lax.all_to_all(ensemble_prediction, 'member', split_axis=2, concat_axis=0...  28.2 us
    reduce_sum x1, other arithmetic, shards(): score_sums = by_axis(jnp.sum(point_score, axis=(1, 2)), SPACE)  5.99 us
    all_to_all x1, starting transfers between devices, shards(): lax.all_to_all(ensemble_prediction, 'member', split_axis=2, concat_axis=0...  5.42 us
    unnamed x6, local copies, waits for them, and re-layouts  4.94 us
    all_to_all x1, starting transfers between devices, sent_to_all(): return lax.all_to_all(copies, axis, split_axis=0, concat_axis=0, tiled=True)  4.64 us
  transfers between devices with their start and end apart: 2, of which 1 were waited for; matrix products, arithmetic and copies ran while one was open for 2% of the time, Pallas kernels for 0%

commit v1 on v0

v1 whole, which is shorter than its diff:
```python
import functools

import jax
import jax.numpy as jnp
from jax import lax
from jax.experimental import pallas as pl
from jax.experimental.pallas import tpu as pltpu
from jax.sharding import Mesh
from jax.sharding import PartitionSpec as P

VARIABLE_NUMBER = 300
ATMOS = 180
TILE_SITES = 128
LON = 720
ROWS = 360
MEMBERS = 4
HALF = VARIABLE_NUMBER // 2
PARTS = 2
STEP = HALF // PARTS
SPACE = ("space_0", "space_1", "space_2", "space_3")
EVERY = ("member", *SPACE)
COEFF = (1.0 - 0.05 / MEMBERS) / (2.0 * MEMBERS * (MEMBERS - 1))
TOP = 32767.0
LEAST_EXPONENT = -120.0

NEAR_FROM_END = [(0, 1), (3, 2)]
FAR_FROM_END = [(0, 2), (3, 1)]
ACROSS = [(1, 2), (2, 1)]
TO_END = [(1, 0), (2, 3)]


def encode_kernel(first_ref, own, near_end, far_end, across, obs, weight, codes, sums, values):
    first = first_ref[0]

    def score(i, top):
        target = obs[i].astype(jnp.float32)
        a = own[i].astype(jnp.float32)
        b = near_end[i].astype(jnp.float32)
        c = far_end[i].astype(jnp.float32)
        d = across[i].astype(jnp.float32)
        skill = jnp.abs(a - target) + jnp.abs(b - target) + jnp.abs(c - target) + jnp.abs(d - target)
        low_ab, high_ab = jnp.minimum(a, b), jnp.maximum(a, b)
        low_cd, high_cd = jnp.minimum(c, d), jnp.maximum(c, d)
        outer = jnp.maximum(high_ab, high_cd) - jnp.minimum(low_ab, low_cd)
        inner = jnp.abs(jnp.minimum(high_ab, high_cd) - jnp.maximum(low_ab, low_cd))
        group = (first + i >= ATMOS).astype(jnp.int32)
        value = (skill * (1.0 / MEMBERS) - (2.0 * COEFF) * (3.0 * outer + inner)) * weight[group]
        values[i] = value
        sums[pl.ds(i, 1), :] = jnp.sum(value, axis=0, keepdims=True)
        return jnp.maximum(top, jnp.abs(value))

    top = lax.fori_loop(0, STEP, score, jnp.zeros(values.shape[1:], jnp.float32), unroll=5)
    top = jnp.broadcast_to(jnp.max(top, keepdims=True), top.shape)
    k = jnp.where(top > 0.0, jnp.ceil(jnp.log2(jnp.where(top > 0.0, top, 1.0))), 0.0)
    k = jnp.maximum(k, LEAST_EXPONENT)
    shrink = jnp.exp2(-k)
    codes[STEP] = k.astype(jnp.int32).astype(codes.dtype)

    def code(i, carry):
        value = values[i]
        root = jnp.sqrt(jnp.sqrt(jnp.abs(value) * shrink))
        steps = jnp.minimum(root * TOP + 0.5, TOP)
        steps = jnp.where(value < 0.0, -steps, steps)
        codes[i] = steps.astype(jnp.int32).astype(codes.dtype)
        return carry

    lax.fori_loop(0, STEP, code, 0, unroll=5)


def encode(first, own, near_end, far_end, across, obs, weight):
    vmem = pl.BlockSpec(memory_space=pltpu.VMEM)
    return pl.pallas_call(
        encode_kernel,
        out_shape=(
            jax.ShapeDtypeStruct((STEP + 1, *obs.shape[1:]), jnp.int16),
            jax.ShapeDtypeStruct((STEP, obs.shape[2]), jnp.float32),
        ),
        in_specs=[pl.BlockSpec(memory_space=pltpu.SMEM)] + [vmem] * 6,
        out_specs=(vmem, vmem),
        scratch_shapes=[pltpu.VMEM(obs.shape, jnp.float32)],
        compiler_params=pltpu.CompilerParams(vmem_limit_bytes=16 << 20),
        cost_estimate=pl.CostEstimate(flops=30 * obs.size, bytes_accessed=14 * obs.size, transcendentals=2 * obs.size),
    )(first, own, near_end, far_end, across, obs, weight)


def decode_kernel(where_ref, scale, mine, sent, out_before, out):
    del out_before
    first = where_ref[0] * STEP

    def channels(codes):
        unit = jnp.exp2(codes[STEP].astype(jnp.float32)) * (1.0 / TOP**4)
        units = (unit * scale[0], unit * scale[1])

        def channel(i, carry):
            steps = codes[i].astype(jnp.float32)
            square = steps * steps
            ocean = first + i >= ATMOS
            out[i] = (steps * jnp.abs(steps)) * square * jnp.where(ocean, units[1], units[0])
            return carry

        lax.fori_loop(0, STEP, channel, 0, unroll=5)

    @pl.when(where_ref[1] == 1)
    def _():
        channels(mine)

    @pl.when(where_ref[1] == 0)
    def _():
        channels(sent)


def decode(where, scale, mine, sent, out):
    rows, sites = mine.shape[1:]
    vmem = pl.BlockSpec(memory_space=pltpu.VMEM)
    shape = jax.ShapeDtypeStruct((VARIABLE_NUMBER, rows, sites), jnp.float32)
    first = out is None
    codes_spec = pl.BlockSpec(mine.shape, lambda g, w: (0, 0, 0))
    kernel = decode_kernel
    if first:
        def kernel(where_ref, scale, mine, sent, out):
            decode_kernel(where_ref, scale, mine, sent, None, out)
    return pl.pallas_call(
        kernel,
        out_shape=shape,
        grid_spec=pltpu.PrefetchScalarGridSpec(
            num_scalar_prefetch=1,
            grid=(1,),
            in_specs=[pl.BlockSpec(memory_space=pltpu.SMEM), codes_spec, codes_spec]
            + ([] if first else [pl.BlockSpec(memory_space=pl.ANY)]),
            out_specs=pl.BlockSpec((STEP, rows, sites), lambda g, w: (w[0], 0, 0)),
        ),
        input_output_aliases={} if first else {4: 0},
        compiler_params=pltpu.CompilerParams(vmem_limit_bytes=16 << 20),
        cost_estimate=pl.CostEstimate(flops=8 * mine.size, bytes_accessed=8 * mine.size, transcendentals=0),
    )(where, scale, mine, sent, *(() if first else (out,)))


def per_channel(values):
    is_ocean = jnp.arange(VARIABLE_NUMBER, dtype=jnp.int32) >= ATMOS
    return jnp.where(is_ocean, values[1], values[0])


def shards(ensemble_prediction, observed_analysis, validity_flags):
    blocks_here = observed_analysis.shape[1]
    member = lax.axis_index("member")
    side = member // 2
    middle = ((member == 1) | (member == 2)).astype(jnp.int32)
    prediction = ensemble_prediction[0]

    def cut(array, half, part):
        return lax.dynamic_slice_in_dim(array, half * HALF + part * STEP, STEP, 0)

    arrived = []
    for part in range(PARTS):
        near, far = cut(prediction, side, part), cut(prediction, 1 - side, part)
        across = lax.ppermute(far, "member", ACROSS)
        far_end = lax.ppermute(far, "member", FAR_FROM_END)
        near_end = lax.ppermute(near, "member", NEAR_FROM_END)
        arrived.append((near, near_end, far_end, across))

    first_point = lax.axis_index(SPACE) * (blocks_here * TILE_SITES)
    position = first_point + jnp.arange(blocks_here * TILE_SITES, dtype=jnp.int32).reshape(
        blocks_here, TILE_SITES
    )
    inside = (position < ROWS * LON).astype(jnp.float32)
    lat_row = (position // LON).astype(jnp.float32)
    cosine = jnp.cos(jnp.pi * ((lat_row + 0.5) / ROWS - 0.5))
    valid = inside[None] * (validity_flags > 0).astype(jnp.float32)
    weight = cosine[None] * valid
    totals = lax.psum(jnp.concatenate([jnp.sum(weight, axis=(1, 2)), jnp.sum(valid, axis=(1, 2))]), SPACE)
    area_sum, count = totals[:2], totals[2:]
    scale = count / area_sum

    out = None
    sums = []
    codes_here = []
    for part in range(PARTS):
        first = side * HALF + part * STEP
        codes, rows = encode(first[None], *arrived[part], cut(observed_analysis, side, part), weight)
        codes_here.append(codes)
        sums.append(rows)
    moved = []
    for part in range(PARTS):
        codes = codes_here[part]
        over = lax.ppermute(codes, "member", ACROSS)
        near_sent = lax.ppermute(codes, "member", TO_END)
        far_sent = lax.ppermute(over, "member", TO_END)
        moved.append((codes, near_sent, over, far_sent))
    for part in range(PARTS):
        codes, near_sent, over, far_sent = moved[part]
        out = decode(jnp.stack([side * PARTS + part, middle]), scale, codes, near_sent, out)
    for part in range(PARTS):
        codes, near_sent, over, far_sent = moved[part]
        out = decode(jnp.stack([(1 - side) * PARTS + part, middle]), scale, over, far_sent, out)

    here = jnp.sum(jnp.concatenate(sums), axis=1)
    here = jnp.where(middle == 1, here, 0.0)
    spread_out = lax.dynamic_update_slice_in_dim(jnp.zeros((VARIABLE_NUMBER,), jnp.float32), here, side * HALF, 0)
    channel_loss = lax.psum(spread_out, EVERY) / per_channel(area_sum)
    return (out, channel_loss)


def solution(mesh):
    split = Mesh(
        mesh.devices.reshape(mesh.shape["member"], 8, 2, 4, 2),
        ("member", "space_0", "space_1", "space_2", "space_3"),
    )
    return jax.shard_map(
        shards,
        mesh=split,
        in_specs=(P("member", None, SPACE, None), P(None, SPACE, None), P(None, SPACE, None)),
        out_specs=(P(None, SPACE, None), P()),
        check_vma=False,
    )
```

time: 162 us -> 571 us (3.52)
  blocking collectives: 102 us -> 531 us
  waiting for transfers between devices: 28.2 us -> 1.74 us
  Pallas kernels: 0 us -> 12.3 us
  starting transfers between devices: 10.1 us -> 18.3 us
  other arithmetic: 10.5 us -> 2.86 us
  local copies, waits for them, and re-layouts: 10.2 us -> 3.14 us
    psum x8 -> x2, blocking collectives: 102 us -> 531 us  [the longest x1 417 us: shards(): lax.psum(jnp.concatenate([jnp.sum(weight, axis=(1, 2)), jnp.sum(valid, ax...]
    all_to_all x2 -> x0, waiting for transfers between devices: 28.2 us -> none  [the longest x1 28.2 us: shards(): lax.all_to_all(ensemble_prediction, 'member', split_axis=2, concat_axis=0...]
    ppermute x0 -> x12, starting transfers between devices: none -> 18.3 us  [the longest x2 6.36 us: shards(): far_end = lax.ppermute(far, 'member', FAR_FROM_END)]
    pallas_call x0 -> x6, Pallas kernels: none -> 12.3 us  [the longest x4 8.75 us: decode(): pl.pallas_call(kernel, out_shape=shape, grid_spec=pltpu.PrefetchScalarGri...]
    all_to_all x2 -> x0, starting transfers between devices: 10.1 us -> none  [the longest x1 5.42 us: shards(): lax.all_to_all(ensemble_prediction, 'member', split_axis=2, concat_axis=0...]
    reduce_sum x3, other arithmetic: 6.2 us -> 0.32 us  [the longest x1 0.11 us: shards(): here = jnp.sum(jnp.concatenate(sums), axis=1)]
  transfers between devices with their start and end apart: 2 -> 12, of which waited for: 1 -> 1; matrix products, arithmetic and copies ran while one was open for 2% -> 1% of each run, Pallas kernels for 0% -> 2%
where the time goes in v1:
time: 571 us; the launch traced here: 570 us
  blocking collectives  531 us (93%)
  starting transfers between devices  18.3 us (3%)
  Pallas kernels  12.3 us (2%)
    psum x1, blocking collectives, shards(): lax.psum(jnp.concatenate([jnp.sum(weight, axis=(1, 2)), jnp.sum(valid, ax...  417 us
    psum x1, blocking collectives, shards(): channel_loss = lax.psum(spread_out, EVERY) / per_channel(area_sum)  114 us
  transfers between devices with their start and end apart: 12, of which 1 were waited for; matrix products, arithmetic and copies ran while one was open for 1% of the time, Pallas kernels for 2%

profile of v1, /device:TPU:1, one launch (start us, length us, event | category | flops | bytes accessed | tf_op | source)
XLA Modules:
  0.0 570.1 jit_solution(10065169023402103022)
XLA Ops:
  0.7 2.4 dynamic-slice_bitcast_fusion
  3.1 5.0 collective-permute-start.6
  8.1 0.7 collective-permute-start.7
  8.8 2.8 collective-permute-start.5
  11.6 1.3 collective-permute-start.1
  13.0 0.1 fusion.9
  13.1 0.1 select_reduce_fusion
  13.2 0.1 pad_maximum_fusion
  13.3 0.7 collective-permute-start.2
  14.0 416.6 %psum.14 = f32[4]{0:T(128)S(1)} all-reduce(f32[4]{0:T(128)S(1)} %pad_maximum_fusion), channel_id=1, replica_groups=mesh['member'=4,'space_0'=8,'space_1'=2,'space_2'=4,'space_3'=2] {'space..., use_global_device_ids=true, to_apply=%region_2.3 | all-reduce | flops 4 | bytes 32 | tf_op jit(solution)/shard_map/psum | solution.py:170
  430.8 1.3 collective-permute-start
  432.1 0.1 pad_add_fusion.1.where_ref
  432.2 0.7 fusion.10
  432.8 0.1 constant_dynamic-slice_fusion
  433.0 1.8 shard_map.51
  434.8 0.7 collective-permute-start.8
  435.5 1.7 collective-permute-done.near_end
  437.2 1.8 shard_map.50
  439.0 0.7 collective-permute-start.3
  439.7 0.1 pad_add_fusion.where_ref
  439.8 1.3 collective-permute-start.11
  441.1 1.3 collective-permute-start.10
  442.4 0.1 maximum_reduce_fusion
  442.5 1.3 collective-permute-start.9
  443.8 1.3 collective-permute-start.4
  445.2 0.1 select_dynamic-update-slice_fusion
  445.3 114.2 %psum.15 = f32[300]{0:T(512)S(1)} all-reduce(f32[300]{0:T(512)S(1)} %select_dynamic-update-slice_fusion), channel_id=1, replica_groups=mesh['member'=4,'space_0'=8,'space_1'=2,'space_2'=4,'space_3'=2] {'membe..., use_global_device_ids=true, to_apply=%region_4.5 | all-reduce | flops 300 | bytes 2400 | tf_op jit(solution)/shard_map/psum | solution.py:199
  559.4 1.9 select_divide_fusion
  561.3 2.2 shard_map.52.out_before
  563.5 2.2 shard_map.53.out_before
  565.7 2.2 shard_map.54.out_before
  567.9 2.2 shard_map.55
  (21 shorter events, 0.3 us)
Async XLA Ops:
  0.6 12.4 %copy-start.1 = (s32[2,16,128]{2,1,0:T(8,128)S(1)}, s32[2,16,128]{2,1,0:T(8,128)}, u32[]{:S(2)}) copy-start(s32[2,16,128]{2,1,0:T(8,128)} %param.5) | copy-start | bytes 49156
  0.6 432.2 %copy-start = (bf16[300,16,128]{2,1,0:T(8,128)(2,1)S(1)}, bf16[300,16,128]{2,1,0:T(8,128)(2,1)}, u32[]{:S(2)}) copy-start(bf16[300,16,128]{2,1,0:T(8,128)(2,1)} %param.4) | copy-start | bytes 3686404
  3.1 429.9 %collective-permute-start.6 = (bf16[75,16,128]{2,1,0:T(8,128)(2,1)}, bf16[75,16,128]{2,1,0:T(8,128)(2,1)S(1)}, u32[]{:S(2)}, u32[]{:S(2)}) collective-permute-start(bf16[75,16,128]{2,1,0:T(8,128)(2,1)} %get-tuple-element.15), channel_id=1, source_target_pairs={{0,256},{384,128},{1,257},{385,129},{2,258},{386,130},{3,259},{387... | collective-permute-start | bytes 921608 | tf_op jit(solution)/shard_map/ppermute | solution.py:157
  8.1 424.9 %collective-permute-start.7 = (bf16[75,16,128]{2,1,0:T(8,128)(2,1)}, bf16[75,16,128]{2,1,0:T(8,128)(2,1)S(1)}, u32[]{:S(2)}, u32[]{:S(2)}) collective-permute-start(bf16[75,16,128]{2,1,0:T(8,128)(2,1)} %get-tuple-element.15), channel_id=1, source_target_pairs={{128,256},{256,128},{129,257},{257,129},{130,258},{258,130},{131,2... | collective-permute-start | bytes 921608 | tf_op jit(solution)/shard_map/ppermute | solution.py:156
  8.8 422.0 %collective-permute-start.5 = (bf16[75,16,128]{2,1,0:T(8,128)(2,1)S(1)}, bf16[75,16,128]{2,1,0:T(8,128)(2,1)S(1)}, u32[]{:S(2)}, u32[]{:S(2)}) collective-permute-start(bf16[75,16,128]{2,1,0:T(8,128)(2,1)S(1)} %get-tuple-element.18.own), channel_id=1, source_target_pairs={{0,128},{384,256},{1,129},{385,257},{2,130},{386,258},{3,131},{387... | collective-permute-start | bytes 921608 | tf_op jit(solution)/shard_map/ppermute | solution.py:158
  11.6 425.6 %collective-permute-start.1 = (bf16[75,16,128]{2,1,0:T(8,128)(2,1)}, bf16[75,16,128]{2,1,0:T(8,128)(2,1)S(1)}, u32[]{:S(2)}, u32[]{:S(2)}) collective-permute-start(bf16[75,16,128]{2,1,0:T(8,128)(2,1)} %get-tuple-element.16), channel_id=1, source_target_pairs={{0,256},{384,128},{1,257},{385,129},{2,258},{386,130},{3,259},{387... | collective-permute-start | bytes 921608 | tf_op jit(solution)/shard_map/ppermute | solution.py:157
  13.3 423.9 %collective-permute-start.2 = (bf16[75,16,128]{2,1,0:T(8,128)(2,1)}, bf16[75,16,128]{2,1,0:T(8,128)(2,1)S(1)}, u32[]{:S(2)}, u32[]{:S(2)}) collective-permute-start(bf16[75,16,128]{2,1,0:T(8,128)(2,1)} %get-tuple-element.16), channel_id=1, source_target_pairs={{128,256},{256,128},{129,257},{257,129},{130,258},{258,130},{131,2... | collective-permute-start | bytes 921608 | tf_op jit(solution)/shard_map/ppermute | solution.py:156
  430.8 6.4 %collective-permute-start = (bf16[75,16,128]{2,1,0:T(8,128)(2,1)S(1)}, bf16[75,16,128]{2,1,0:T(8,128)(2,1)S(1)}, u32[]{:S(2)}, u32[]{:S(2)}) collective-permute-start(bf16[75,16,128]{2,1,0:T(8,128)(2,1)S(1)} %get-tuple-element.17.own), channel_id=1, source_target_pairs={{0,128},{384,256},{1,129},{385,257},{2,130},{386,258},{3,131},{387... | collective-permute-start | bytes 921608 | tf_op jit(solution)/shard_map/ppermute | solution.py:158
  434.8 7.8 %collective-permute-start.8 = (s16[76,16,128]{2,1,0:T(8,128)(2,1)S(1)}, s16[76,16,128]{2,1,0:T(8,128)(2,1)S(1)}, u32[]{:S(2)}, u32[]{:S(2)}) collective-permute-start(s16[76,16,128]{2,1,0:T(8,128)(2,1)S(1)} %get-tuple-element.7.mine), channel_id=1, source_target_pairs={{128,256},{256,128},{129,257},{257,129},{130,258},{258,130},{131,2... | collective-permute-start | bytes 933896 | tf_op jit(solution)/shard_map/ppermute | solution.py:185
  439.0 4.9 collective-permute-start.3
  439.8 121.5 %collective-permute-start.11 = (s16[76,16,128]{2,1,0:T(8,128)(2,1)S(1)}, s16[76,16,128]{2,1,0:T(8,128)(2,1)S(1)}, u32[]{:S(2)}, u32[]{:S(2)}) collective-permute-start(s16[76,16,128]{2,1,0:T(8,128)(2,1)S(1)} %get-tuple-element.7.mine), channel_id=1, source_target_pairs={{128,0},{256,384},{129,1},{257,385},{130,2},{258,386},{131,3},{259... | collective-permute-start | bytes 933896 | tf_op jit(solution)/shard_map/ppermute | solution.py:186
  441.1 122.4 %collective-permute-start.10 = (s16[76,16,128]{2,1,0:T(8,128)(2,1)S(1)}, s16[76,16,128]{2,1,0:T(8,128)(2,1)S(1)}, u32[]{:S(2)}, u32[]{:S(2)}) collective-permute-start(s16[76,16,128]{2,1,0:T(8,128)(2,1)S(1)} %get-tuple-element.6.mine), channel_id=1, source_target_pairs={{128,0},{256,384},{129,1},{257,385},{130,2},{258,386},{131,3},{259... | collective-permute-start | bytes 933896 | tf_op jit(solution)/shard_map/ppermute | solution.py:186
  442.5 123.2 %collective-permute-start.9 = (s16[76,16,128]{2,1,0:T(8,128)(2,1)S(1)}, s16[76,16,128]{2,1,0:T(8,128)(2,1)S(1)}, u32[]{:S(2)}, u32[]{:S(2)}) collective-permute-start(s16[76,16,128]{2,1,0:T(8,128)(2,1)S(1)} %collective-permute-done.8.mine), channel_id=1, source_target_pairs={{128,0},{256,384},{129,1},{257,385},{130,2},{258,386},{131,3},{259... | collective-permute-start | bytes 933896 | tf_op jit(solution)/shard_map/ppermute | solution.py:187
  443.8 124.0 %collective-permute-start.4 = (s16[76,16,128]{2,1,0:T(8,128)(2,1)S(1)}, s16[76,16,128]{2,1,0:T(8,128)(2,1)S(1)}, u32[]{:S(2)}, u32[]{:S(2)}) collective-permute-start(s16[76,16,128]{2,1,0:T(8,128)(2,1)S(1)} %collective-permute-done.3.mine), channel_id=1, source_target_pairs={{128,0},{256,384},{129,1},{257,385},{130,2},{258,386},{131,3},{259... | collective-permute-start | bytes 933896 | tf_op jit(solution)/shard_map/ppermute | solution.py:187

commit v2 on v0

v2 whole, which is shorter than its diff:
```python
import jax
import jax.numpy as jnp
from jax import lax
from jax.experimental import pallas as pl
from jax.experimental.pallas import tpu as pltpu
from jax.sharding import Mesh
from jax.sharding import PartitionSpec as P

VARIABLE_NUMBER = 300
ATMOS = 180
TILE_SITES = 128
LON = 720
ROWS = 360
MEMBERS = 4
SHARE = VARIABLE_NUMBER // MEMBERS
SPACE = ("space_0", "space_1", "space_2", "space_3")
ALONG_ZX = ("space_0", "space_2", "space_3")
ALONG_Y = ("member", "space_1")
COEFF = (1.0 - 0.05 / MEMBERS) / (2.0 * MEMBERS * (MEMBERS - 1))
TOP = 32767.0
LEAST_EXPONENT = -120.0


def encode_kernel(member, forecasts, obs, weight, codes, partial, values, rows):
    first = member[0] * SHARE

    def score(i, top):
        target = obs[i].astype(jnp.float32)
        a, b, c, d = (forecasts[m, i].astype(jnp.float32) for m in range(MEMBERS))
        skill = jnp.abs(a - target) + jnp.abs(b - target) + jnp.abs(c - target) + jnp.abs(d - target)
        low_ab, high_ab = jnp.minimum(a, b), jnp.maximum(a, b)
        low_cd, high_cd = jnp.minimum(c, d), jnp.maximum(c, d)
        outer = jnp.maximum(high_ab, high_cd) - jnp.minimum(low_ab, low_cd)
        inner = jnp.abs(jnp.minimum(high_ab, high_cd) - jnp.maximum(low_ab, low_cd))
        group = (first + i >= ATMOS).astype(jnp.int32)
        value = (skill * (1.0 / MEMBERS) - (2.0 * COEFF) * (3.0 * outer + inner)) * weight[group]
        values[i] = value
        rows[pl.ds(i, 1), :] = jnp.sum(value, axis=0, keepdims=True)
        return jnp.maximum(top, jnp.abs(value))

    rows[...] = jnp.zeros(rows.shape, jnp.float32)
    top = lax.fori_loop(0, SHARE, score, jnp.zeros(values.shape[1:], jnp.float32), unroll=5)
    for g in range(2):
        rows[SHARE + g : SHARE + g + 1, :] = jnp.sum(weight[g], axis=0, keepdims=True)
        valid = (weight[g] > 0.0).astype(jnp.float32)
        rows[SHARE + 2 + g : SHARE + 3 + g, :] = jnp.sum(valid, axis=0, keepdims=True)
    ones = jnp.ones((8, TILE_SITES), jnp.float32)
    partial[...] = lax.dot_general(
        ones, rows[...], (((1,), (1,)), ((), ())), precision=lax.Precision.HIGHEST, preferred_element_type=jnp.float32
    )

    top = jnp.broadcast_to(jnp.max(top, keepdims=True), top.shape)
    k = jnp.where(top > 0.0, jnp.ceil(jnp.log2(jnp.where(top > 0.0, top, 1.0))), 0.0)
    k = jnp.maximum(k, LEAST_EXPONENT)
    shrink = jnp.exp2(-k)
    exponent = k.astype(jnp.int32).astype(codes.dtype)
    for m in range(MEMBERS):
        codes[m, SHARE] = exponent

    def code(i, carry):
        value = values[i]
        root = jnp.sqrt(jnp.sqrt(jnp.abs(value) * shrink))
        steps = jnp.minimum(root * TOP + 0.5, TOP)
        steps = jnp.where(value < 0.0, -steps, steps).astype(jnp.int32).astype(codes.dtype)
        for m in range(MEMBERS):
            codes[m, i] = steps
        return carry

    lax.fori_loop(0, SHARE, code, 0, unroll=5)


def encode(member, forecasts, obs, weight):
    blocks, sites = obs.shape[1:]
    share = (SHARE, blocks, sites)
    return pl.pallas_call(
        encode_kernel,
        out_shape=(
            jax.ShapeDtypeStruct((MEMBERS, SHARE + 1, blocks, sites), jnp.int16),
            jax.ShapeDtypeStruct((8, sites), jnp.float32),
        ),
        grid_spec=pltpu.PrefetchScalarGridSpec(
            num_scalar_prefetch=1,
            grid=(1,),
            in_specs=[
                pl.BlockSpec((MEMBERS, *share), lambda g, m: (0, 0, 0, 0)),
                pl.BlockSpec(share, lambda g, m: (m[0], 0, 0)),
                pl.BlockSpec(weight.shape, lambda g, m: (0, 0, 0)),
            ],
            out_specs=(
                pl.BlockSpec((MEMBERS, SHARE + 1, blocks, sites), lambda g, m: (0, 0, 0, 0)),
                pl.BlockSpec((8, sites), lambda g, m: (0, 0)),
            ),
            scratch_shapes=[pltpu.VMEM(share, jnp.float32), pltpu.VMEM((sites, sites), jnp.float32)],
        ),
        compiler_params=pltpu.CompilerParams(vmem_limit_bytes=24 << 20),
        cost_estimate=pl.CostEstimate(
            flops=30 * SHARE * blocks * sites, bytes_accessed=14 * SHARE * blocks * sites, transcendentals=0
        ),
    )(member, forecasts, obs, weight)


def decode_kernel(scale, codes, out):
    first = pl.program_id(0) * SHARE
    unit = jnp.exp2(codes[0, SHARE].astype(jnp.float32)) * (1.0 / TOP**4)

    def channel(i, carry):
        steps = codes[0, i].astype(jnp.float32)
        square = steps * steps
        group = (first + i >= ATMOS).astype(jnp.int32)
        out[i] = (steps * jnp.abs(steps)) * square * (unit * scale[group])
        return carry

    lax.fori_loop(0, SHARE, channel, 0, unroll=5)


def decode(scale, codes):
    blocks, sites = codes.shape[2:]
    return pl.pallas_call(
        decode_kernel,
        out_shape=jax.ShapeDtypeStruct((VARIABLE_NUMBER, blocks, sites), jnp.float32),
        grid=(MEMBERS,),
        in_specs=[
            pl.BlockSpec(memory_space=pltpu.SMEM),
            pl.BlockSpec((1, SHARE + 1, blocks, sites), lambda m: (m, 0, 0, 0)),
        ],
        out_specs=pl.BlockSpec((SHARE, blocks, sites), lambda m: (m, 0, 0)),
        compiler_params=pltpu.CompilerParams(vmem_limit_bytes=24 << 20),
        cost_estimate=pl.CostEstimate(
            flops=8 * codes.size, bytes_accessed=6 * codes.size, transcendentals=0
        ),
    )(scale, codes)


def from_each(row, axes):
    copies = jnp.broadcast_to(row[None], (lax.axis_size(axes), *row.shape))
    return lax.all_to_all(copies, axes, split_axis=0, concat_axis=0, tiled=True)


def shards(ensemble_prediction, observed_analysis, validity_flags):
    blocks_here = observed_analysis.shape[1]
    forecasts = lax.all_to_all(ensemble_prediction[0], "member", split_axis=0, concat_axis=0, tiled=True)
    forecasts = forecasts.reshape(MEMBERS, SHARE, *forecasts.shape[1:])

    first_point = lax.axis_index(SPACE) * (blocks_here * TILE_SITES)
    position = first_point + jnp.arange(blocks_here * TILE_SITES, dtype=jnp.int32).reshape(
        blocks_here, TILE_SITES
    )
    inside = (position < ROWS * LON).astype(jnp.float32)
    lat_row = (position // LON).astype(jnp.float32)
    cosine = jnp.cos(jnp.pi * ((lat_row + 0.5) / ROWS - 0.5))
    weight = (cosine * inside)[None] * (validity_flags > 0).astype(jnp.float32)

    member = lax.axis_index("member")[None]
    codes, partial = encode(member, forecasts, observed_analysis, weight)
    gathered = lax.all_to_all(codes, "member", split_axis=0, concat_axis=0, tiled=True)

    over_zx = jnp.sum(from_each(partial[:1], ALONG_ZX), axis=0)
    over_y = from_each(over_zx, ALONG_Y).reshape(MEMBERS, -1, TILE_SITES)
    totals = jnp.sum(over_y, axis=1)
    area_sum = totals[0, SHARE : SHARE + 2]
    count = totals[0, SHARE + 2 : SHARE + 4]
    point_score = decode(count / area_sum, gathered)
    by_member = jnp.arange(VARIABLE_NUMBER, dtype=jnp.int32) >= ATMOS
    channel_loss = totals[:, :SHARE].reshape(VARIABLE_NUMBER) / jnp.where(by_member, area_sum[1], area_sum[0])
    return (point_score, channel_loss)


def solution(mesh):
    split = Mesh(
        mesh.devices.reshape(mesh.shape["member"], 8, 2, 4, 2),
        ("member", "space_0", "space_1", "space_2", "space_3"),
    )
    return jax.shard_map(
        shards,
        mesh=split,
        in_specs=(P("member", None, SPACE, None), P(None, SPACE, None), P(None, SPACE, None)),
        out_specs=(P(None, SPACE, None), P()),
        check_vma=False,
    )
```

time: 162 us -> 111 us (0.69)
  blocking collectives: 102 us -> 37.1 us
  waiting for transfers between devices: 28.2 us -> 54.6 us
  local copies, waits for them, and re-layouts: 10.2 us -> 0.77 us
  other arithmetic: 10.5 us -> 2.02 us
  Pallas kernels: 0 us -> 5.89 us
    psum x8 -> x0, blocking collectives: 102 us -> none  [by_axis(): return functools.reduce(lax.psum, axes, x)]
    all_to_all x0 -> x2, blocking collectives: none -> 37.1 us  [from_each(): return lax.all_to_all(copies, axes, split_axis=0, concat_axis=0, tiled=True)]
    all_to_all x2, waiting for transfers between devices: 28.2 us -> 54.6 us  [the longest x1 27.9 us: shards(): lax.all_to_all(ensemble_prediction[0], 'member', split_axis=0, concat_axi...]
    reduce_sum x3 -> x2, other arithmetic: 6.2 us -> 0.04 us  [the longest x1 0.02 us: shards(): over_zx = jnp.sum(from_each(partial[:1], ALONG_ZX), axis=0)]
    pallas_call x0 -> x2, Pallas kernels: none -> 5.89 us  [the longest x1 2.97 us: decode(): pl.pallas_call(decode_kernel, out_shape=jax.ShapeDtypeStruct((VARIABLE_NU...]
    unnamed x6 -> x4, local copies, waits for them, and re-layouts: 4.94 us -> 0.01 us
    transpose x1 -> x0, local copies, waits for them, and re-layouts: 1.86 us -> none  [laid_out(): blocks = jnp.moveaxis(blocks, 0, dim)]
    broadcast_in_dim x1 -> x3, local copies, waits for them, and re-layouts: 1.75 us -> 0.03 us  [from_each(): copies = jnp.broadcast_to(row[None], (lax.axis_size(axes), *row.shape))]
  transfers between devices with their start and end apart: 2 -> 2, of which waited for: 1 -> 2; matrix products, arithmetic and copies ran while one was open for 2% -> 2% of each run, Pallas kernels for 0% -> 0%
where the time goes in v2:
time: 111 us; the launch traced here: 110 us
  waiting for transfers between devices  54.6 us (49%)
  blocking collectives  37.1 us (33%)
  starting transfers between devices  9.1 us (8%)
  Pallas kernels  5.89 us (5%)
  other arithmetic  2.02 us (2%)
    all_to_all x2, blocking collectives, from_each(): return lax.all_to_all(copies, axes, split_axis=0, concat_axis=0, tiled=True)  37.1 us
    all_to_all x1, waiting for transfers between devices, shards(): lax.all_to_all(ensemble_prediction[0], 'member', split_axis=0, concat_axi...  27.9 us
    all_to_all x1, waiting for transfers between devices, shards(): lax.all_to_all(codes, 'member', split_axis=0, concat_axis=0, tiled=True)  26.7 us
    all_to_all x1, starting transfers between devices, shards(): lax.all_to_all(ensemble_prediction[0], 'member', split_axis=0, concat_axi...  5.56 us
    all_to_all x1, starting transfers between devices, shards(): lax.all_to_all(codes, 'member', split_axis=0, concat_axis=0, tiled=True)  3.54 us
    pallas_call x1, Pallas kernels, decode(): pl.pallas_call(decode_kernel, out_shape=jax.ShapeDtypeStruct((VARIABLE_NU...  2.97 us
    pallas_call x1, Pallas kernels, encode(): pl.pallas_call(encode_kernel, out_shape=(jax.ShapeDtypeStruct((MEMBERS, S...  2.91 us
  transfers between devices with their start and end apart: 2, of which 2 were waited for; matrix products, arithmetic and copies ran while one was open for 2% of the time, Pallas kernels for 0%

profile of v2, /device:TPU:1, one launch (start us, length us, event | category | flops | bytes accessed | tf_op | source)
XLA Modules:
  0.0 110.2 jit_solution(7704707691898483838)
XLA Ops:
  0.6 0.0 copy-start.1
  0.6 0.0 copy-start
  0.6 5.6 %all-to-all-start = ((bf16[300,16,128]{2,1,0:T(8,128)(2,1)}), bf16[300,16,128]{2,1,0:T(8,128)(2,1)S(1)}, u32[]{:S(2)}, u32[]{:S(2)}) async-start(bf16[300,16,128]{2,1,0:T(8,128)(2,1)} %bitcast.13), calls=%async_computation | async-start | bytes 2457600 | tf_op jit(solution)/shard_map/all_to_all | solution.py:141
  6.2 0.1 fusion.6
  6.3 0.0 copy-done.1
  6.3 27.9 %all-to-all-done = bf16[300,16,128]{2,1,0:T(8,128)(2,1)S(1)} async-done(((bf16[300,16,128]{2,1,0:T(8,128)(2,1)}), bf16[300,16,128]{2,1,0:T(8,128)(2,1)S(1)}, u32[]{:S(2)}, u32[]{:S(2)}) %all-to-all-start) | async-done | bytes 1228832 | tf_op jit(solution)/shard_map/all_to_all | solution.py:141
  34.2 0.0 copy-done
  34.2 2.9 %shard_map.50 = (s16[4,76,16,128]{3,2,1,0:T(8,128)(2,1)}, f32[8,128]{1,0:T(8,128)S(1)}) custom-call(s32[1]{0:T(128)} %bitcast.member, bf16[4,75,16,128]{3,2,1,0:T(8,128)(2,1)S(1)} %bitcast.12, bf16[300,16,128]{2,1,0:T(8,128)(2,1)S(1)} %copy-done, f32[2,16,128]{2,1,0:T(8,128)S(1)} %compare_select_fusion.weight), custom_call_target="tpu_custom_call" | custom-call | flops 4608000 | bytes 2150400 | tf_op jit(solution)/shard_map/pallas_call | solution.py:75
  37.1 25.1 %all_to_all.20 = f32[64,1,128]{2,1,0:T(1,128)S(1)} all-to-all(f32[64,1,128]{2,1,0:T(1,128)S(1)} %broadcast_in_dim.28), channel_id=1, replica_groups=mesh['member'=4,'space_0'=8,'space_1'=2,'space_2'=4,'space_3'=2] {'space..., dimensions={0} | all-to-all | bytes 65536 | tf_op jit(solution)/shard_map/all_to_all | solution.py:136
  62.2 12.0 %all_to_all.21 = f32[8,1,128]{2,1,0:T(1,128)S(1)} all-to-all(f32[8,1,128]{2,1,0:T(1,128)S(1)} %broadcast_in_dim.29), channel_id=1, replica_groups=mesh['member'=4,'space_0'=8,'space_1'=2,'space_2'=4,'space_3'=2] {'membe..., dimensions={0} | all-to-all | bytes 8192 | tf_op jit(solution)/shard_map/all_to_all | solution.py:136
  74.3 3.5 %all-to-all-start.3 = ((s16[4,76,16,128]{3,2,1,0:T(8,128)(2,1)}), s16[4,76,16,128]{3,2,1,0:T(8,128)(2,1)S(1)}, u32[]{:S(2)}, u32[]{:S(2)}) async-start(s16[4,76,16,128]{3,2,1,0:T(8,128)(2,1)} %get-tuple-element.5), calls=%async_computation.3 | async-start | bytes 2490368 | tf_op jit(solution)/shard_map/all_to_all | solution.py:155
  77.8 0.1 reshape.63
  77.9 0.6 fusion.10
  78.6 0.1 fusion.9.scale
  78.6 1.8 %select_divide_fusion = f32[300]{0:T(512)} fusion(f32[300]{0:T(512)S(1)} %reshape.63, f32[]{:T(128)} %bitcast.8, f32[]{:T(128)} %bitcast.7), kind=kLoop, calls=%fused_computation.14 | loop fusion | flops 900 | bytes 2408 | tf_op jit(solution)/shard_map/div | solution.py:164
  80.5 26.7 %all-to-all-done.3.codes = s16[4,76,16,128]{3,2,1,0:T(8,128)(2,1)S(1)} async-done(((s16[4,76,16,128]{3,2,1,0:T(8,128)(2,1)}), s16[4,76,16,128]{3,2,1,0:T(8,128)(2,1)S(1)}, u32[]{:S(2)}, u32[]{:S(2)}) %all-to-all-start.3) | async-done | bytes 1245216 | tf_op jit(solution)/shard_map/all_to_all | solution.py:155
  107.2 3.0 %shard_map.51 = f32[300,16,128]{2,1,0:T(8,128)} custom-call(f32[2]{0:T(128)S(1)} %fusion.9.scale, s16[4,76,16,128]{3,2,1,0:T(8,128)(2,1)S(1)} %all-to-all-done.3.codes), custom_call_target="tpu_custom_call" | custom-call | flops 4980736 | bytes 3735552 | tf_op jit(solution)/shard_map/pallas_call | solution.py:118
  (6 shorter events, 0.1 us)
Async XLA Ops:
  0.6 5.7 %copy-start.1 = (s32[2,16,128]{2,1,0:T(8,128)S(1)}, s32[2,16,128]{2,1,0:T(8,128)}, u32[]{:S(2)}) copy-start(s32[2,16,128]{2,1,0:T(8,128)} %param.5) | copy-start | bytes 49156
  0.6 33.5 %copy-start = (bf16[300,16,128]{2,1,0:T(8,128)(2,1)S(1)}, bf16[300,16,128]{2,1,0:T(8,128)(2,1)}, u32[]{:S(2)}) copy-start(bf16[300,16,128]{2,1,0:T(8,128)(2,1)} %obs.1) | copy-start | bytes 3686404
  0.6 33.5 %all-to-all-start = ((bf16[300,16,128]{2,1,0:T(8,128)(2,1)}), bf16[300,16,128]{2,1,0:T(8,128)(2,1)S(1)}, u32[]{:S(2)}, u32[]{:S(2)}) async-start(bf16[300,16,128]{2,1,0:T(8,128)(2,1)} %bitcast.13), calls=%async_computation | async-start | bytes 2457600 | tf_op jit(solution)/shard_map/all_to_all | solution.py:141
  74.3 32.9 %all-to-all-start.3 = ((s16[4,76,16,128]{3,2,1,0:T(8,128)(2,1)}), s16[4,76,16,128]{3,2,1,0:T(8,128)(2,1)S(1)}, u32[]{:S(2)}, u32[]{:S(2)}) async-start(s16[4,76,16,128]{3,2,1,0:T(8,128)(2,1)} %get-tuple-element.5), calls=%async_computation.3 | async-start | bytes 2490368 | tf_op jit(solution)/shard_map/all_to_all | solution.py:155

commit v3 on v2

--- a/solution.py
+++ b/solution.py
@@ -19,6 +19,7 @@
 COEFF = (1.0 - 0.05 / MEMBERS) / (2.0 * MEMBERS * (MEMBERS - 1))
 TOP = 32767.0
 LEAST_EXPONENT = -120.0
+PAIRS = (SHARE + 1) // 2
 
 
 def encode_kernel(member, forecasts, obs, weight, codes, partial, values, rows):
@@ -53,20 +54,18 @@
     k = jnp.where(top > 0.0, jnp.ceil(jnp.log2(jnp.where(top > 0.0, top, 1.0))), 0.0)
     k = jnp.maximum(k, LEAST_EXPONENT)
     shrink = jnp.exp2(-k)
-    exponent = k.astype(jnp.int32).astype(codes.dtype)
-    for m in range(MEMBERS):
-        codes[m, SHARE] = exponent
-
-    def code(i, carry):
-        value = values[i]
+
+    def code(value):
         root = jnp.sqrt(jnp.sqrt(jnp.abs(value) * shrink))
         steps = jnp.minimum(root * TOP + 0.5, TOP)
-        steps = jnp.where(value < 0.0, -steps, steps).astype(jnp.int32).astype(codes.dtype)
-        for m in range(MEMBERS):
-            codes[m, i] = steps
+        return jnp.where(value < 0.0, -steps, steps).astype(jnp.int32)
+
+    def pair(i, carry):
+        codes[i] = (code(values[PAIRS + i]) << 16) | (code(values[i]) & 0xFFFF)
         return carry
 
-    lax.fori_loop(0, SHARE, code, 0, unroll=5)
+    lax.fori_loop(0, PAIRS - 1, pair, 0, unroll=4)
+    codes[PAIRS - 1] = (k.astype(jnp.int32) << 16) | (code(values[PAIRS - 1]) & 0xFFFF)
 
 
 def encode(member, forecasts, obs, weight):
@@ -75,7 +74,7 @@
     return pl.pallas_call(
         encode_kernel,
         out_shape=(
-            jax.ShapeDtypeStruct((MEMBERS, SHARE + 1, blocks, sites), jnp.int16),
+            jax.ShapeDtypeStruct((PAIRS, blocks, sites), jnp.int32),
             jax.ShapeDtypeStruct((8, sites), jnp.float32),
         ),
         grid_spec=pltpu.PrefetchScalarGridSpec(
@@ -87,7 +86,7 @@
                 pl.BlockSpec(weight.shape, lambda g, m: (0, 0, 0)),
             ],
             out_specs=(
-                pl.BlockSpec((MEMBERS, SHARE + 1, blocks, sites), lambda g, m: (0, 0, 0, 0)),
+                pl.BlockSpec((PAIRS, blocks, sites), lambda g, m: (0, 0, 0)),
                 pl.BlockSpec((8, sites), lambda g, m: (0, 0)),
             ),
             scratch_shapes=[pltpu.VMEM(share, jnp.float32), pltpu.VMEM((sites, sites), jnp.float32)],
@@ -99,36 +98,74 @@
     )(member, forecasts, obs, weight)
 
 
-def decode_kernel(scale, codes, out):
-    first = pl.program_id(0) * SHARE
-    unit = jnp.exp2(codes[0, SHARE].astype(jnp.float32)) * (1.0 / TOP**4)
-
-    def channel(i, carry):
-        steps = codes[0, i].astype(jnp.float32)
+def decode_kernel(sums, codes, out, loss, scale, units):
+    step = pl.program_id(0)
+
+    @pl.when(step == 0)
+    def _():
+        halves = sums.shape[0] // MEMBERS
+        totals = [sum(sums[m * halves + h] for h in range(halves)) for m in range(MEMBERS)]
+        lane = lax.broadcasted_iota(jnp.int32, totals[0].shape, 1)
+
+        def at(i):
+            return jnp.sum(jnp.where(lane == i, totals[0], 0.0), keepdims=True)
+
+        area = [at(SHARE + g) for g in range(2)]
+        for g in range(2):
+            scale[g] = jnp.broadcast_to(at(SHARE + 2 + g) / area[g], scale.shape[1:])
+        width = 3 * TILE_SITES
+        channel = lax.broadcasted_iota(jnp.int32, (1, width), 1)
+        wide = jnp.zeros((1, width), jnp.float32)
+        blank = jnp.zeros((1, width - TILE_SITES), jnp.float32)
+        for m in range(MEMBERS):
+            moved = pltpu.roll(jnp.concatenate([totals[m], blank], axis=1), m * SHARE, 1)
+            wide = jnp.where((channel >= m * SHARE) & (channel < (m + 1) * SHARE), moved, wide)
+        loss[...] = wide / jnp.where(channel >= ATMOS, area[1], area[0])
+
+    first = step * SHARE
+    unit = jnp.exp2((codes[PAIRS - 1] >> 16).astype(jnp.float32)) * (1.0 / TOP**4)
+    for g in range(2):
+        units[g] = unit * scale[g]
+
+    def write(i, code):
+        steps = code.astype(jnp.float32)
         square = steps * steps
         group = (first + i >= ATMOS).astype(jnp.int32)
-        out[i] = (steps * jnp.abs(steps)) * square * (unit * scale[group])
+        out[i] = (steps * jnp.abs(steps)) * square * units[group]
+
+    def pair(i, carry):
+        both = codes[i]
+        write(i, (both << 16) >> 16)
+        write(PAIRS + i, both >> 16)
         return carry
 
-    lax.fori_loop(0, SHARE, channel, 0, unroll=5)
-
-
-def decode(scale, codes):
-    blocks, sites = codes.shape[2:]
+    lax.fori_loop(0, PAIRS - 1, pair, 0, unroll=4)
+    write(PAIRS - 1, (codes[PAIRS - 1] << 16) >> 16)
+
+
+def decode(sums, codes):
+    blocks, sites = codes.shape[1:]
     return pl.pallas_call(
         decode_kernel,
-        out_shape=jax.ShapeDtypeStruct((VARIABLE_NUMBER, blocks, sites), jnp.float32),
+        out_shape=(
+            jax.ShapeDtypeStruct((VARIABLE_NUMBER, blocks, sites), jnp.float32),
+            jax.ShapeDtypeStruct((1, 3 * sites), jnp.float32),
+        ),
         grid=(MEMBERS,),
         in_specs=[
-            pl.BlockSpec(memory_space=pltpu.SMEM),
-            pl.BlockSpec((1, SHARE + 1, blocks, sites), lambda m: (m, 0, 0, 0)),
+            pl.BlockSpec(sums.shape, lambda m: (0, 0, 0)),
+            pl.BlockSpec((PAIRS, blocks, sites), lambda m: (m, 0, 0)),
         ],
-        out_specs=pl.BlockSpec((SHARE, blocks, sites), lambda m: (m, 0, 0)),
+        out_specs=(
+            pl.BlockSpec((SHARE, blocks, sites), lambda m: (m, 0, 0)),
+            pl.BlockSpec((1, 3 * sites), lambda m: (0, 0)),
+        ),
+        scratch_shapes=[pltpu.VMEM((2, blocks, sites), jnp.float32)] * 2,
         compiler_params=pltpu.CompilerParams(vmem_limit_bytes=24 << 20),
         cost_estimate=pl.CostEstimate(
-            flops=8 * codes.size, bytes_accessed=6 * codes.size, transcendentals=0
-        ),
-    )(scale, codes)
+            flops=16 * codes.size, bytes_accessed=12 * codes.size, transcendentals=0
+        ),
+    )(sums, codes)
 
 
 def from_each(row, axes):
@@ -152,17 +189,10 @@
 
     member = lax.axis_index("member")[None]
     codes, partial = encode(member, forecasts, observed_analysis, weight)
-    gathered = lax.all_to_all(codes, "member", split_axis=0, concat_axis=0, tiled=True)
-
+    gathered = lax.all_gather(codes, "member", tiled=True)
     over_zx = jnp.sum(from_each(partial[:1], ALONG_ZX), axis=0)
-    over_y = from_each(over_zx, ALONG_Y).reshape(MEMBERS, -1, TILE_SITES)
-    totals = jnp.sum(over_y, axis=1)
-    area_sum = totals[0, SHARE : SHARE + 2]
-    count = totals[0, SHARE + 2 : SHARE + 4]
-    point_score = decode(count / area_sum, gathered)
-    by_member = jnp.arange(VARIABLE_NUMBER, dtype=jnp.int32) >= ATMOS
-    channel_loss = totals[:, :SHARE].reshape(VARIABLE_NUMBER) / jnp.where(by_member, area_sum[1], area_sum[0])
-    return (point_score, channel_loss)
+    point_score, loss = decode(from_each(over_zx, ALONG_Y), gathered)
+    return (point_score, loss[0, :VARIABLE_NUMBER])
 
 
 def solution(mesh):

time: 111 us -> 99.3 us (0.89)
  waiting for transfers between devices: 54.6 us -> 35.3 us
  between operations: 0.68 us -> 14.1 us
  starting transfers between devices: 9.1 us -> 5.57 us
  other arithmetic: 2.02 us -> 0.1 us
  local copies, waits for them, and re-layouts: 0.77 us -> 1.92 us
    all_to_all x1 -> x0, waiting for transfers between devices: 26.7 us -> none  [shards(): lax.all_to_all(codes, 'member', split_axis=0, concat_axis=0, tiled=True)]
    all_gather x0 -> x1, waiting for transfers between devices: none -> 7.48 us  [shards(): gathered = lax.all_gather(codes, 'member', tiled=True)]
    all_to_all x1 -> x0, starting transfers between devices: 3.54 us -> none  [shards(): lax.all_to_all(codes, 'member', split_axis=0, concat_axis=0, tiled=True)]
    div x2 -> x0, other arithmetic: 1.9 us -> none  [the longest x1 1.83 us: shards(): totals[:, :SHARE].reshape(VARIABLE_NUMBER)]
    unnamed x4 -> x6, local copies, waits for them, and re-layouts: 0.01 us -> 1.3 us
  transfers between devices with their start and end apart: 2 -> 2, of which waited for: 2 -> 2; matrix products, arithmetic and copies ran while one was open for 2% -> 0% of each run, Pallas kernels for 0% -> 0%
where the time goes in v3:
time: 99.3 us; the launch traced here: 99 us
  blocking collectives  37.1 us (37%)
  waiting for transfers between devices  35.3 us (36%)
  between operations  14.1 us (14%)
  starting transfers between devices  5.57 us (6%)
  Pallas kernels  4.87 us (5%)
  local copies, waits for them, and re-layouts  1.92 us (2%)
    all_to_all x2, blocking collectives, from_each(): return lax.all_to_all(copies, axes, split_axis=0, concat_axis=0, tiled=True)  37.1 us
    all_to_all x1, waiting for transfers between devices, shards(): lax.all_to_all(ensemble_prediction[0], 'member', split_axis=0, concat_axi...  27.8 us
    all_gather x1, waiting for transfers between devices, shards(): gathered = lax.all_gather(codes, 'member', tiled=True)  7.48 us
    all_to_all x1, starting transfers between devices, shards(): lax.all_to_all(ensemble_prediction[0], 'member', split_axis=0, concat_axi...  5.56 us
    pallas_call x1, Pallas kernels, encode(): pl.pallas_call(encode_kernel, out_shape=(jax.ShapeDtypeStruct((PAIRS, blo...  2.48 us
    pallas_call x1, Pallas kernels, decode(): pl.pallas_call(decode_kernel, out_shape=(jax.ShapeDtypeStruct((VARIABLE_N...  2.39 us
  transfers between devices with their start and end apart: 2, of which 2 were waited for; matrix products, arithmetic and copies ran while one was open for 0% of the time, Pallas kernels for 0%

profile of v3, /device:TPU:1, one launch (start us, length us, event | category | flops | bytes accessed | tf_op | source)
XLA Modules:
  0.0 99.0 jit_solution(8599843927675791398)
XLA Ops:
  7.2 0.0 copy-start.2
  7.2 0.0 copy-start.1
  7.2 5.6 %all-to-all-start = ((bf16[300,16,128]{2,1,0:T(8,128)(2,1)}), bf16[300,16,128]{2,1,0:T(8,128)(2,1)S(1)}, u32[]{:S(2)}, u32[]{:S(2)}) async-start(bf16[300,16,128]{2,1,0:T(8,128)(2,1)} %bitcast.7), calls=%async_computation | async-start | bytes 2457600 | tf_op jit(solution)/shard_map/all_to_all | solution.py:178
  12.7 0.0 all-gather.2.cloned.1.call-start
  12.8 0.1 fusion.6
  12.8 0.0 copy-done.2
  12.8 27.8 %all-to-all-done = bf16[300,16,128]{2,1,0:T(8,128)(2,1)S(1)} async-done(((bf16[300,16,128]{2,1,0:T(8,128)(2,1)}), bf16[300,16,128]{2,1,0:T(8,128)(2,1)S(1)}, u32[]{:S(2)}, u32[]{:S(2)}) %all-to-all-start) | async-done | bytes 1228832 | tf_op jit(solution)/shard_map/all_to_all | solution.py:178
  40.7 0.0 copy-done.1
  40.7 2.5 %shard_map.50 = (s32[38,16,128]{2,1,0:T(8,128)}, f32[8,128]{1,0:T(8,128)S(1)}) custom-call(s32[1]{0:T(128)} %bitcast.member, bf16[4,75,16,128]{3,2,1,0:T(8,128)(2,1)S(1)} %bitcast.6, bf16[300,16,128]{2,1,0:T(8,128)(2,1)S(1)} %copy-done.1, f32[2,16,128]{2,1,0:T(8,128)S(1)} %compare_select_fusion.weight), custom_call_target="tpu_custom_call" | custom-call | flops 4608000 | bytes 2150400 | tf_op jit(solution)/shard_map/pallas_call | solution.py:74
  43.2 0.0 all-gather.2.cloned.1.call-update
  43.2 25.1 %all_to_all.15 = f32[64,1,128]{2,1,0:T(1,128)S(1)} all-to-all(f32[64,1,128]{2,1,0:T(1,128)S(1)} %broadcast_in_dim.20), channel_id=1, replica_groups=mesh['member'=4,'space_0'=8,'space_1'=2,'space_2'=4,'space_3'=2] {'space..., dimensions={0} | all-to-all | bytes 65536 | tf_op jit(solution)/shard_map/all_to_all | solution.py:173
  68.4 12.0 %all_to_all.16.sums = f32[8,1,128]{2,1,0:T(1,128)S(1)} all-to-all(f32[8,1,128]{2,1,0:T(1,128)S(1)} %broadcast_in_dim.21), channel_id=1, replica_groups=mesh['member'=4,'space_0'=8,'space_1'=2,'space_2'=4,'space_3'=2] {'membe..., dimensions={0} | all-to-all | bytes 8192 | tf_op jit(solution)/shard_map/all_to_all | solution.py:173
  80.4 7.5 %all-gather.2.cloned.1.call-done.codes = s32[152,16,128]{2,1,0:T(8,128)} async-done(((s32[38,16,128]{2,1,0:T(8,128)}), s32[152,16,128]{2,1,0:T(8,128)}) %all-gather.2.cloned.1.call-update) | async-done | bytes 1245200 | tf_op jit(solution)/shard_map/all_gather | solution.py:192
  87.9 0.0 copy-start
  87.9 1.3 %copy-done = s32[152,16,128]{2,1,0:T(8,128)S(1)} copy-done((s32[152,16,128]{2,1,0:T(8,128)S(1)}, s32[152,16,128]{2,1,0:T(8,128)}, u32[]{:S(2)}) %copy-start) | copy-done | bytes 1245208
  89.2 2.4 %shard_map.51 = (f32[300,16,128]{2,1,0:T(8,128)}, f32[1,384]{1,0:T(1,128)S(1)}) custom-call(f32[8,1,128]{2,1,0:T(1,128)S(1)} %all_to_all.16.sums, s32[152,16,128]{2,1,0:T(8,128)S(1)} %copy-done), custom_call_target="tpu_custom_call" | custom-call | flops 4980736 | bytes 3735552 | tf_op jit(solution)/shard_map/pallas_call | solution.py:148
  91.6 0.6 slice_reduce_fusion
  (5 shorter events, 0.1 us)
Async XLA Ops:
  7.2 5.7 %copy-start.2 = (s32[2,16,128]{2,1,0:T(8,128)S(1)}, s32[2,16,128]{2,1,0:T(8,128)}, u32[]{:S(2)}) copy-start(s32[2,16,128]{2,1,0:T(8,128)} %param.5) | copy-start | bytes 49156
  7.2 33.5 %copy-start.1 = (bf16[300,16,128]{2,1,0:T(8,128)(2,1)S(1)}, bf16[300,16,128]{2,1,0:T(8,128)(2,1)}, u32[]{:S(2)}) copy-start(bf16[300,16,128]{2,1,0:T(8,128)(2,1)} %obs.1) | copy-start | bytes 3686404
  7.2 33.5 %all-to-all-start = ((bf16[300,16,128]{2,1,0:T(8,128)(2,1)}), bf16[300,16,128]{2,1,0:T(8,128)(2,1)S(1)}, u32[]{:S(2)}, u32[]{:S(2)}) async-start(bf16[300,16,128]{2,1,0:T(8,128)(2,1)} %bitcast.7), calls=%async_computation | async-start | bytes 2457600 | tf_op jit(solution)/shard_map/all_to_all | solution.py:178
  12.7 75.2 %all-gather.2.cloned.1.call-start = ((), (), s32[]{:S(2)}) async-start(), calls=%async_computation.3 | async-start | bytes 1556480 | tf_op jit(solution)/shard_map/all_gather | solution.py:192
  87.9 1.3 %copy-start = (s32[152,16,128]{2,1,0:T(8,128)S(1)}, s32[152,16,128]{2,1,0:T(8,128)}, u32[]{:S(2)}) copy-start(s32[152,16,128]{2,1,0:T(8,128)} %all-gather.2.cloned.1.call-done.codes) | copy-start | bytes 3735556
Sparse Core Ops, SparseCore 0:
  43.3 44.5 all-gather.1

commit v4 on v3

--- a/solution.py
+++ b/solution.py
@@ -18,6 +18,8 @@
 ALONG_Y = ("member", "space_1")
 COEFF = (1.0 - 0.05 / MEMBERS) / (2.0 * MEMBERS * (MEMBERS - 1))
 TOP = 32767.0
+BESIDE = [(m, m ^ 1) for m in range(MEMBERS)]
+ACROSS = [(m, m ^ 2) for m in range(MEMBERS)]
 LEAST_EXPONENT = -120.0
 PAIRS = (SHARE + 1) // 2
 
@@ -26,7 +28,7 @@
     first = member[0] * SHARE
 
     def score(i, top):
-        target = obs[i].astype(jnp.float32)
+        target = obs[first + i].astype(jnp.float32)
         a, b, c, d = (forecasts[m, i].astype(jnp.float32) for m in range(MEMBERS))
         skill = jnp.abs(a - target) + jnp.abs(b - target) + jnp.abs(c - target) + jnp.abs(d - target)
         low_ab, high_ab = jnp.minimum(a, b), jnp.maximum(a, b)
@@ -71,26 +73,16 @@
 def encode(member, forecasts, obs, weight):
     blocks, sites = obs.shape[1:]
     share = (SHARE, blocks, sites)
+    vmem = pl.BlockSpec(memory_space=pltpu.VMEM)
     return pl.pallas_call(
         encode_kernel,
         out_shape=(
             jax.ShapeDtypeStruct((PAIRS, blocks, sites), jnp.int32),
             jax.ShapeDtypeStruct((8, sites), jnp.float32),
         ),
-        grid_spec=pltpu.PrefetchScalarGridSpec(
-            num_scalar_prefetch=1,
-            grid=(1,),
-            in_specs=[
-                pl.BlockSpec((MEMBERS, *share), lambda g, m: (0, 0, 0, 0)),
-                pl.BlockSpec(share, lambda g, m: (m[0], 0, 0)),
-                pl.BlockSpec(weight.shape, lambda g, m: (0, 0, 0)),
-            ],
-            out_specs=(
-                pl.BlockSpec((PAIRS, blocks, sites), lambda g, m: (0, 0, 0)),
-                pl.BlockSpec((8, sites), lambda g, m: (0, 0)),
-            ),
-            scratch_shapes=[pltpu.VMEM(share, jnp.float32), pltpu.VMEM((sites, sites), jnp.float32)],
-        ),
+        in_specs=[pl.BlockSpec(memory_space=pltpu.SMEM), vmem, vmem, vmem],
+        out_specs=(vmem, vmem),
+        scratch_shapes=[pltpu.VMEM(share, jnp.float32), pltpu.VMEM((sites, sites), jnp.float32)],
         compiler_params=pltpu.CompilerParams(vmem_limit_bytes=24 << 20),
         cost_estimate=pl.CostEstimate(
             flops=30 * SHARE * blocks * sites, bytes_accessed=14 * SHARE * blocks * sites, transcendentals=0
@@ -98,11 +90,13 @@
     )(member, forecasts, obs, weight)
 
 
-def decode_kernel(sums, codes, out, loss, scale, units):
+def decode_kernel(member, sums, own, beside, across, corner, out, loss, scale, units, held, copied):
     step = pl.program_id(0)
+    copy = pltpu.make_async_copy(corner, held, copied)
 
     @pl.when(step == 0)
     def _():
+        copy.start()
         halves = sums.shape[0] // MEMBERS
         totals = [sum(sums[m * halves + h] for h in range(halves)) for m in range(MEMBERS)]
         lane = lax.broadcasted_iota(jnp.int32, totals[0].shape, 1)
@@ -120,57 +114,75 @@
         for m in range(MEMBERS):
             moved = pltpu.roll(jnp.concatenate([totals[m], blank], axis=1), m * SHARE, 1)
             wide = jnp.where((channel >= m * SHARE) & (channel < (m + 1) * SHARE), moved, wide)
-        loss[...] = wide / jnp.where(channel >= ATMOS, area[1], area[0])
-
-    first = step * SHARE
-    unit = jnp.exp2((codes[PAIRS - 1] >> 16).astype(jnp.float32)) * (1.0 / TOP**4)
-    for g in range(2):
-        units[g] = unit * scale[g]
-
-    def write(i, code):
-        steps = code.astype(jnp.float32)
-        square = steps * steps
-        group = (first + i >= ATMOS).astype(jnp.int32)
-        out[i] = (steps * jnp.abs(steps)) * square * units[group]
-
-    def pair(i, carry):
-        both = codes[i]
-        write(i, (both << 16) >> 16)
-        write(PAIRS + i, both >> 16)
-        return carry
-
-    lax.fori_loop(0, PAIRS - 1, pair, 0, unroll=4)
-    write(PAIRS - 1, (codes[PAIRS - 1] << 16) >> 16)
-
-
-def decode(sums, codes):
-    blocks, sites = codes.shape[1:]
+        wide = wide / jnp.where(channel >= ATMOS, area[1], area[0])
+        loss[...] = wide[0, :VARIABLE_NUMBER]
+
+    first = (member[0] ^ step) * SHARE
+
+    def share(codes):
+        unit = jnp.exp2((codes[PAIRS - 1] >> 16).astype(jnp.float32)) * (1.0 / TOP**4)
+        for g in range(2):
+            units[g] = unit * scale[g]
+
+        def write(i, code):
+            steps = code.astype(jnp.float32)
+            square = steps * steps
+            group = (first + i >= ATMOS).astype(jnp.int32)
+            out[i] = (steps * jnp.abs(steps)) * square * units[group]
+
+        def pair(i, carry):
+            both = codes[i]
+            write(i, (both << 16) >> 16)
+            write(PAIRS + i, both >> 16)
+            return carry
+
+        lax.fori_loop(0, PAIRS - 1, pair, 0, unroll=4)
+        write(PAIRS - 1, (codes[PAIRS - 1] << 16) >> 16)
+
+    for s, codes in enumerate((own, beside, across, held)):
+
+        @pl.when(step == s)
+        def _(s=s, codes=codes):
+            if s == MEMBERS - 1:
+                copy.wait()
+            share(codes)
+
+
+def decode(member, sums, shares):
+    blocks, sites = shares[0].shape[1:]
+    vmem = pl.BlockSpec(memory_space=pltpu.VMEM)
     return pl.pallas_call(
         decode_kernel,
         out_shape=(
             jax.ShapeDtypeStruct((VARIABLE_NUMBER, blocks, sites), jnp.float32),
-            jax.ShapeDtypeStruct((1, 3 * sites), jnp.float32),
-        ),
-        grid=(MEMBERS,),
-        in_specs=[
-            pl.BlockSpec(sums.shape, lambda m: (0, 0, 0)),
-            pl.BlockSpec((PAIRS, blocks, sites), lambda m: (m, 0, 0)),
-        ],
-        out_specs=(
-            pl.BlockSpec((SHARE, blocks, sites), lambda m: (m, 0, 0)),
-            pl.BlockSpec((1, 3 * sites), lambda m: (0, 0)),
-        ),
-        scratch_shapes=[pltpu.VMEM((2, blocks, sites), jnp.float32)] * 2,
+            jax.ShapeDtypeStruct((VARIABLE_NUMBER,), jnp.float32),
+        ),
+        grid_spec=pltpu.PrefetchScalarGridSpec(
+            num_scalar_prefetch=1,
+            grid=(MEMBERS,),
+            in_specs=[vmem] * 4 + [pl.BlockSpec(memory_space=pl.ANY)],
+            out_specs=(
+                pl.BlockSpec((SHARE, blocks, sites), lambda s, member: (member[0] ^ s, 0, 0)),
+                pl.BlockSpec((VARIABLE_NUMBER,), lambda s, member: (0,)),
+            ),
+            scratch_shapes=[pltpu.VMEM((2, blocks, sites), jnp.float32)] * 2
+            + [pltpu.VMEM(shares[0].shape, jnp.int32), pltpu.SemaphoreType.DMA],
+        ),
         compiler_params=pltpu.CompilerParams(vmem_limit_bytes=24 << 20),
         cost_estimate=pl.CostEstimate(
-            flops=16 * codes.size, bytes_accessed=12 * codes.size, transcendentals=0
-        ),
-    )(sums, codes)
+            flops=64 * shares[0].size, bytes_accessed=48 * shares[0].size, transcendentals=0
+        ),
+    )(member, sums, *shares)
 
 
 def from_each(row, axes):
     copies = jnp.broadcast_to(row[None], (lax.axis_size(axes), *row.shape))
     return lax.all_to_all(copies, axes, split_axis=0, concat_axis=0, tiled=True)
+
+
+def in_one_step(always, f, *args):
+    shapes = jax.eval_shape(f, *args)
+    return lax.cond(always, f, lambda *args: jax.tree.map(lambda x: jnp.zeros(x.shape, x.dtype), shapes), *args)
 
 
 def shards(ensemble_prediction, observed_analysis, validity_flags):
@@ -189,10 +201,18 @@
 
     member = lax.axis_index("member")[None]
     codes, partial = encode(member, forecasts, observed_analysis, weight)
-    gathered = lax.all_gather(codes, "member", tiled=True)
-    over_zx = jnp.sum(from_each(partial[:1], ALONG_ZX), axis=0)
-    point_score, loss = decode(from_each(over_zx, ALONG_Y), gathered)
-    return (point_score, loss[0, :VARIABLE_NUMBER])
+    always = member[0] >= 0
+    across = lax.ppermute(codes, "member", ACROSS)
+    beside = lax.ppermute(codes, "member", BESIDE)
+    over_zx = in_one_step(always, lambda row: jnp.sum(from_each(row, ALONG_ZX), axis=0), partial[:1])
+
+    def last_step(across, row):
+        corner = lax.ppermute(across, "member", BESIDE)
+        return corner, in_one_step(always, lambda row: from_each(row, ALONG_Y), row)
+
+    corner, over_y = in_one_step(always, last_step, across, over_zx)
+    point_score, loss = decode(member, over_y, (codes, beside, across, corner))
+    return (point_score, loss)
 
 
 def solution(mesh):

time: 99.3 us -> 84.8 us (0.85)
  between operations: 14.1 us -> 0.69 us
  waiting for transfers between devices: 35.3 us -> 27.9 us
  starting transfers between devices: 5.57 us -> 11.3 us
  blocking collectives: 37.1 us -> 39.4 us
  local copies, waits for them, and re-layouts: 1.92 us -> 0.03 us
    all_gather x1 -> x0, waiting for transfers between devices: 7.48 us -> none  [shards(): gathered = lax.all_gather(codes, 'member', tiled=True)]
    ppermute x0 -> x3, starting transfers between devices: none -> 5.76 us  [the longest x1 1.92 us: last_step(): corner = lax.ppermute(across, 'member', BESIDE)]
    all_to_all x2, blocking collectives: 37.1 us -> 39.4 us  [from_each(): return lax.all_to_all(copies, axes, split_axis=0, concat_axis=0, tiled=True)]
    unnamed x6 -> x4, local copies, waits for them, and re-layouts: 1.3 us -> 0.01 us
  transfers between devices with their start and end apart: 2 -> 4, of which waited for: 2 -> 1; matrix products, arithmetic and copies ran while one was open for 0% -> 0% of each run, Pallas kernels for 0% -> 0%
where the time goes in v4:
time: 84.8 us; the launch traced here: 84.4 us
  blocking collectives  39.4 us (46%)
  waiting for transfers between devices  27.9 us (33%)
  starting transfers between devices  11.3 us (13%)
  Pallas kernels  4.93 us (6%)
    all_to_all x2, blocking collectives, from_each(): return lax.all_to_all(copies, axes, split_axis=0, concat_axis=0, tiled=True)  39.4 us
    all_to_all x1, waiting for transfers between devices, shards(): lax.all_to_all(ensemble_prediction[0], 'member', split_axis=0, concat_axi...  27.9 us
    all_to_all x1, starting transfers between devices, shards(): lax.all_to_all(ensemble_prediction[0], 'member', split_axis=0, concat_axi...  5.56 us
    pallas_call x1, Pallas kernels, decode(): pl.pallas_call(decode_kernel, out_shape=(jax.ShapeDtypeStruct((VARIABLE_N...  3.17 us
    ppermute x1, starting transfers between devices, last_step(): corner = lax.ppermute(across, 'member', BESIDE)  1.92 us
    ppermute x1, starting transfers between devices, shards(): across = lax.ppermute(codes, 'member', ACROSS)  1.92 us
    ppermute x1, starting transfers between devices, shards(): beside = lax.ppermute(codes, 'member', BESIDE)  1.92 us
    pallas_call x1, Pallas kernels, encode(): pl.pallas_call(encode_kernel, out_shape=(jax.ShapeDtypeStruct((PAIRS, blo...  1.76 us
  transfers between devices with their start and end apart: 4, of which 1 were waited for; matrix products, arithmetic and copies ran while one was open for 0% of the time, Pallas kernels for 0%

profile of v4, /device:TPU:1, one launch (start us, length us, event | category | flops | bytes accessed | tf_op | source)
XLA Modules:
  0.0 84.4 jit_solution(2394818685063276198)
XLA Ops:
  0.6 0.0 copy-start.1
  0.6 0.0 copy-start
  0.6 5.6 %all-to-all-start.2 = ((bf16[300,16,128]{2,1,0:T(8,128)(2,1)}), bf16[300,16,128]{2,1,0:T(8,128)(2,1)S(1)}, u32[]{:S(2)}, u32[]{:S(2)}) async-start(bf16[300,16,128]{2,1,0:T(8,128)(2,1)} %bitcast.9), calls=%async_computation.2 | async-start | bytes 2457600 | tf_op jit(solution)/shard_map/all_to_all | solution.py:190
  6.2 0.1 fusion.6
  6.3 0.0 copy-done.1
  6.3 27.9 %all-to-all-done.2 = bf16[300,16,128]{2,1,0:T(8,128)(2,1)S(1)} async-done(((bf16[300,16,128]{2,1,0:T(8,128)(2,1)}), bf16[300,16,128]{2,1,0:T(8,128)(2,1)S(1)}, u32[]{:S(2)}, u32[]{:S(2)}) %all-to-all-start.2) | async-done | bytes 1228832 | tf_op jit(solution)/shard_map/all_to_all | solution.py:190
  34.2 0.0 copy-done
  34.2 1.8 %shard_map.50 = (s32[38,16,128]{2,1,0:T(8,128)S(1)}, f32[8,128]{1,0:T(8,128)S(1)}) custom-call(s32[1]{0:T(128)} %bitcast.4.member, bf16[4,75,16,128]{3,2,1,0:T(8,128)(2,1)S(1)} %bitcast.8, bf16[300,16,128]{2,1,0:T(8,128)(2,1)S(1)} %copy-done, f32[2,16,128]{2,1,0:T(8,128)S(1)} %compare_select_fusion.weight), custom_call_target="tpu_custom_call" | custom-call | flops 4608000 | bytes 2150400 | tf_op jit(solution)/shard_map/pallas_call | solution.py:77
  35.9 1.9 %collective-permute-start.1 = (s32[38,16,128]{2,1,0:T(8,128)S(1)}, s32[38,16,128]{2,1,0:T(8,128)S(1)}, u32[]{:S(2)}, u32[]{:S(2)}) collective-permute-start(s32[38,16,128]{2,1,0:T(8,128)S(1)} %get-tuple-element.24.own), channel_id=1, source_target_pairs={{0,256},{128,384},{256,0},{384,128},{1,257},{129,385},{257,1},{385... | collective-permute-start | bytes 933896 | tf_op jit(solution)/shard_map/ppermute | solution.py:205
  37.9 1.9 %collective-permute-start.2 = (s32[38,16,128]{2,1,0:T(8,128)S(1)}, s32[38,16,128]{2,1,0:T(8,128)S(1)}, u32[]{:S(2)}, u32[]{:S(2)}) collective-permute-start(s32[38,16,128]{2,1,0:T(8,128)S(1)} %get-tuple-element.24.own), channel_id=1, source_target_pairs={{0,128},{128,0},{256,384},{384,256},{1,129},{129,1},{257,385},{385... | collective-permute-start | bytes 933896 | tf_op jit(solution)/shard_map/ppermute | solution.py:206
  39.8 27.2 %conditional.3 = (f32[1,128]{1,0:T(1,128)S(1)}) conditional(s32[]{:T(128)} %convert_element_type.16, () %tuple.28, f32[8,128]{1,0:T(8,128)S(1)} %get-tuple-element.25), branch_computations={%region_0.1_spmd, %region_1.3_spmd} | conditional | flops 8064 | bytes 133132 | solution.py:185
  39.8 27.1 %all_to_all.13 = f32[64,1,128]{2,1,0:T(1,128)S(1)} all-to-all(f32[64,1,128]{2,1,0:T(1,128)S(1)} %broadcast_in_dim.10), channel_id=1, replica_groups=mesh['member'=4,'space_0'=8,'space_1'=2,'space_2'=4,'space_3'=2] {'space..., dimensions={0} | all-to-all | bytes 65536 | tf_op jit(solution)/shard_map/cond/branch_1_fun/all_to_all | solution.py:180
  67.0 0.0 collective-permute-done.1.across
  67.0 14.2 %conditional.4 = (s32[38,16,128]{2,1,0:T(8,128)}, f32[8,1,128]{2,1,0:T(1,128)}) conditional(s32[]{:T(128)} %convert_element_type.16, () %tuple.27, (s32[38,16,128]{2,1,0:T(8,128)S(1)}, pred[]{:T(512)}, f32[1,128]{1,0:T(1,128)S(1)}) %tuple.29), branch_computations={%region_3.4_spmd, %region_4.7_spmd} | conditional | flops 1 | bytes 1258053 | solution.py:185
  67.0 1.9 %collective-permute-start = (s32[38,16,128]{2,1,0:T(8,128)S(1)}, s32[38,16,128]{2,1,0:T(8,128)}, u32[]{:S(2)}, u32[]{:S(2)}) collective-permute-start(s32[38,16,128]{2,1,0:T(8,128)S(1)} %get-tuple-element.15), channel_id=1, source_target_pairs={{0,128},{128,0},{256,384},{384,256},{1,129},{129,1},{257,385},{385... | collective-permute-start | bytes 933896 | tf_op jit(solution)/shard_map/cond/branch_1_fun/ppermute | solution.py:210
  68.9 12.3 %conditional = (f32[8,1,128]{2,1,0:T(1,128)}) conditional(s32[]{:T(128)} %convert_element_type.13, () %tuple.21, f32[1,128]{1,0:T(1,128)S(1)} %get-tuple-element.17), branch_computations={%region_5.5_spmd, %region_6.6_spmd} | conditional | bytes 12808 | solution.py:185
  68.9 12.3 %all_to_all.14 = f32[8,1,128]{2,1,0:T(1,128)} all-to-all(f32[8,1,128]{2,1,0:T(1,128)S(1)} %broadcast_in_dim.12), channel_id=1, replica_groups=mesh['member'=4,'space_0'=8,'space_1'=2,'space_2'=4,'space_3'=2] {'membe..., dimensions={0} | all-to-all | bytes 8192 | tf_op jit(solution)/shard_map/cond/branch_1_fun/cond/branch_1_fun/all_to_all | solution.py:180
  81.2 0.0 collective-permute-done
  81.2 0.0 collective-permute-done.2.beside
  81.2 3.2 %shard_map.51 = (f32[300,16,128]{2,1,0:T(8,128)}, f32[300]{0:T(512)}) custom-call(s32[1]{0:T(128)} %bitcast.4.member, f32[8,1,128]{2,1,0:T(1,128)} %get-tuple-element.26.sums, s32[38,16,128]{2,1,0:T(8,128)S(1)} %get-tuple-element.24.own, s32[38,16,128]{2,1,0:T(8,128)S(1)} %collective-permute-done.2.beside, s32[38,16,128]{2,1,0:T(8,128)S(1)} %collective-permute-done.1.across, ...), custom_call_target="tpu_custom_call" | custom-call | flops 4980736 | bytes 3735552 | tf_op jit(solution)/shard_map/pallas_call | solution.py:154
  (5 shorter events, 0.1 us)
Async XLA Ops:
  0.6 5.7 %copy-start.1 = (s32[2,16,128]{2,1,0:T(8,128)S(1)}, s32[2,16,128]{2,1,0:T(8,128)}, u32[]{:S(2)}) copy-start(s32[2,16,128]{2,1,0:T(8,128)} %param.11) | copy-start | bytes 49156
  0.6 33.5 %copy-start = (bf16[300,16,128]{2,1,0:T(8,128)(2,1)S(1)}, bf16[300,16,128]{2,1,0:T(8,128)(2,1)}, u32[]{:S(2)}) copy-start(bf16[300,16,128]{2,1,0:T(8,128)(2,1)} %obs.1) | copy-start | bytes 3686404
  0.6 33.5 %all-to-all-start.2 = ((bf16[300,16,128]{2,1,0:T(8,128)(2,1)}), bf16[300,16,128]{2,1,0:T(8,128)(2,1)S(1)}, u32[]{:S(2)}, u32[]{:S(2)}) async-start(bf16[300,16,128]{2,1,0:T(8,128)(2,1)} %bitcast.9), calls=%async_computation.2 | async-start | bytes 2457600 | tf_op jit(solution)/shard_map/all_to_all | solution.py:190
  35.9 31.0 %collective-permute-start.1 = (s32[38,16,128]{2,1,0:T(8,128)S(1)}, s32[38,16,128]{2,1,0:T(8,128)S(1)}, u32[]{:S(2)}, u32[]{:S(2)}) collective-permute-start(s32[38,16,128]{2,1,0:T(8,128)S(1)} %get-tuple-element.24.own), channel_id=1, source_target_pairs={{0,256},{128,384},{256,0},{384,128},{1,257},{129,385},{257,1},{385... | collective-permute-start | bytes 933896 | tf_op jit(solution)/shard_map/ppermute | solution.py:205
  37.9 43.3 %collective-permute-start.2 = (s32[38,16,128]{2,1,0:T(8,128)S(1)}, s32[38,16,128]{2,1,0:T(8,128)S(1)}, u32[]{:S(2)}, u32[]{:S(2)}) collective-permute-start(s32[38,16,128]{2,1,0:T(8,128)S(1)} %get-tuple-element.24.own), channel_id=1, source_target_pairs={{0,128},{128,0},{256,384},{384,256},{1,129},{129,1},{257,385},{385... | collective-permute-start | bytes 933896 | tf_op jit(solution)/shard_map/ppermute | solution.py:206
  67.0 14.2 %collective-permute-start = (s32[38,16,128]{2,1,0:T(8,128)S(1)}, s32[38,16,128]{2,1,0:T(8,128)}, u32[]{:S(2)}, u32[]{:S(2)}) collective-permute-start(s32[38,16,128]{2,1,0:T(8,128)S(1)} %get-tuple-element.15), channel_id=1, source_target_pairs={{0,128},{128,0},{256,384},{384,256},{1,129},{129,1},{257,385},{385... | collective-permute-start | bytes 933896 | tf_op jit(solution)/shard_map/cond/branch_1_fun/ppermute | solution.py:210

commit v5 on v4

--- a/solution.py
+++ b/solution.py
@@ -20,6 +20,8 @@
 TOP = 32767.0
 BESIDE = [(m, m ^ 1) for m in range(MEMBERS)]
 ACROSS = [(m, m ^ 2) for m in range(MEMBERS)]
+CORNER = [(m, m ^ 3) for m in range(MEMBERS)]
+REPEATS = 5
 LEAST_EXPONENT = -120.0
 PAIRS = (SHARE + 1) // 2
 
@@ -90,34 +92,43 @@
     )(member, forecasts, obs, weight)
 
 
-def decode_kernel(member, sums, own, beside, across, corner, out, loss, scale, units, held, copied):
+def in_order(step):
+    return (step & 1) * 2 + (step >> 1)
+
+
+def decode_kernel(member, sums, own, across, beside, corner, out, loss, scale, units, held, copied):
     step = pl.program_id(0)
-    copy = pltpu.make_async_copy(corner, held, copied)
+    halves = sums.shape[0] // MEMBERS
+    copies = [pltpu.make_async_copy(codes, held.at[s], copied.at[s]) for s, codes in enumerate((beside, corner))]
+
+    def total(m):
+        return sum(sums[m * halves + h] for h in range(halves))
+
+    def at(i):
+        row = total(0)
+        lane = lax.broadcasted_iota(jnp.int32, row.shape, 1)
+        return jnp.sum(jnp.where(lane == i, row, 0.0), keepdims=True)
 
     @pl.when(step == 0)
     def _():
-        copy.start()
-        halves = sums.shape[0] // MEMBERS
-        totals = [sum(sums[m * halves + h] for h in range(halves)) for m in range(MEMBERS)]
-        lane = lax.broadcasted_iota(jnp.int32, totals[0].shape, 1)
-
-        def at(i):
-            return jnp.sum(jnp.where(lane == i, totals[0], 0.0), keepdims=True)
-
-        area = [at(SHARE + g) for g in range(2)]
+        for copy in copies:
+            copy.start()
         for g in range(2):
-            scale[g] = jnp.broadcast_to(at(SHARE + 2 + g) / area[g], scale.shape[1:])
+            scale[g] = jnp.broadcast_to(at(SHARE + 2 + g) / at(SHARE + g), scale.shape[1:])
+
+    @pl.when(step == 1)
+    def _():
         width = 3 * TILE_SITES
         channel = lax.broadcasted_iota(jnp.int32, (1, width), 1)
         wide = jnp.zeros((1, width), jnp.float32)
         blank = jnp.zeros((1, width - TILE_SITES), jnp.float32)
         for m in range(MEMBERS):
-            moved = pltpu.roll(jnp.concatenate([totals[m], blank], axis=1), m * SHARE, 1)
+            moved = pltpu.roll(jnp.concatenate([total(m), blank], axis=1), m * SHARE, 1)
             wide = jnp.where((channel >= m * SHARE) & (channel < (m + 1) * SHARE), moved, wide)
-        wide = wide / jnp.where(channel >= ATMOS, area[1], area[0])
+        wide = wide / jnp.where(channel >= ATMOS, at(SHARE + 1), at(SHARE))
         loss[...] = wide[0, :VARIABLE_NUMBER]
 
-    first = (member[0] ^ step) * SHARE
+    first = (member[0] ^ in_order(step)) * SHARE
 
     def share(codes):
         unit = jnp.exp2((codes[PAIRS - 1] >> 16).astype(jnp.float32)) * (1.0 / TOP**4)
@@ -139,12 +150,12 @@
         lax.fori_loop(0, PAIRS - 1, pair, 0, unroll=4)
         write(PAIRS - 1, (codes[PAIRS - 1] << 16) >> 16)
 
-    for s, codes in enumerate((own, beside, across, held)):
+    for s, codes in enumerate((own, across, held.at[0], held.at[1])):
 
         @pl.when(step == s)
         def _(s=s, codes=codes):
-            if s == MEMBERS - 1:
-                copy.wait()
+            if s >= 2:
+                copies[s - 2].wait()
             share(codes)
 
 
@@ -160,13 +171,13 @@
         grid_spec=pltpu.PrefetchScalarGridSpec(
             num_scalar_prefetch=1,
             grid=(MEMBERS,),
-            in_specs=[vmem] * 4 + [pl.BlockSpec(memory_space=pl.ANY)],
+            in_specs=[vmem] * 3 + [pl.BlockSpec(memory_space=pl.ANY)] * 2,
             out_specs=(
-                pl.BlockSpec((SHARE, blocks, sites), lambda s, member: (member[0] ^ s, 0, 0)),
+                pl.BlockSpec((SHARE, blocks, sites), lambda s, member: (member[0] ^ in_order(s), 0, 0)),
                 pl.BlockSpec((VARIABLE_NUMBER,), lambda s, member: (0,)),
             ),
             scratch_shapes=[pltpu.VMEM((2, blocks, sites), jnp.float32)] * 2
-            + [pltpu.VMEM(shares[0].shape, jnp.int32), pltpu.SemaphoreType.DMA],
+            + [pltpu.VMEM((2, *shares[0].shape), jnp.int32), pltpu.SemaphoreType.DMA((2,))],
         ),
         compiler_params=pltpu.CompilerParams(vmem_limit_bytes=24 << 20),
         cost_estimate=pl.CostEstimate(
@@ -175,8 +186,11 @@
     )(member, sums, *shares)
 
 
-def from_each(row, axes):
-    copies = jnp.broadcast_to(row[None], (lax.axis_size(axes), *row.shape))
+def copied(row, number):
+    return jnp.broadcast_to(row[None], (number, *row.shape))
+
+
+def exchanged(copies, axes):
     return lax.all_to_all(copies, axes, split_axis=0, concat_axis=0, tiled=True)
 
 
@@ -203,15 +217,17 @@
     codes, partial = encode(member, forecasts, observed_analysis, weight)
     always = member[0] >= 0
     across = lax.ppermute(codes, "member", ACROSS)
-    beside = lax.ppermute(codes, "member", BESIDE)
-    over_zx = in_one_step(always, lambda row: jnp.sum(from_each(row, ALONG_ZX), axis=0), partial[:1])
-
-    def last_step(across, row):
-        corner = lax.ppermute(across, "member", BESIDE)
-        return corner, in_one_step(always, lambda row: from_each(row, ALONG_Y), row)
-
-    corner, over_y = in_one_step(always, last_step, across, over_zx)
-    point_score, loss = decode(member, over_y, (codes, beside, across, corner))
+
+    def add_up_and_send(codes, copies):
+        beside = lax.ppermute(codes, "member", BESIDE)
+        corner = lax.ppermute(codes, "member", CORNER)
+        over_zx = jnp.sum(exchanged(copies, ALONG_ZX)[::REPEATS], axis=0)
+        over_zx = copied(over_zx, lax.axis_size(ALONG_Y))
+        return beside, corner, in_one_step(always, lambda copies: exchanged(copies, ALONG_Y), over_zx)
+
+    copies = copied(partial[:1], REPEATS * lax.axis_size(ALONG_ZX))
+    beside, corner, over_y = in_one_step(always, add_up_and_send, codes, copies)
+    point_score, loss = decode(member, over_y, (codes, across, beside, corner))
     return (point_score, loss)
 
 

time: 84.8 us -> 82.8 us (0.976)
  blocking collectives: 39.4 us -> 12.7 us
  starting transfers between devices: 11.3 us -> 30.1 us
  waiting for transfers between devices: 27.9 us -> 32.8 us
    all_to_all x2 -> x1, blocking collectives: 39.4 us -> 12.7 us  [exchanged(): return lax.all_to_all(copies, axes, split_axis=0, concat_axis=0, tiled=True)]
    all_to_all x0 -> x1, starting transfers between devices: none -> 15.9 us  [exchanged(): return lax.all_to_all(copies, axes, split_axis=0, concat_axis=0, tiled=True)]
    all_to_all x0 -> x1, waiting for transfers between devices: none -> 4.94 us  [exchanged(): return lax.all_to_all(copies, axes, split_axis=0, concat_axis=0, tiled=True)]
    ppermute x2, starting transfers between devices: 3.84 us -> 6.74 us  [the longest x1 3.64 us: add_up_and_send(): beside = lax.ppermute(codes, 'member', BESIDE)]
  transfers between devices with their start and end apart: 4 -> 5, of which waited for: 1 -> 2; matrix products, arithmetic and copies ran while one was open for 0% -> 1% of each run, Pallas kernels for 0% -> 0%
where the time goes in v5:
time: 82.8 us; the launch traced here: 82.4 us
  waiting for transfers between devices  32.8 us (40%)
  starting transfers between devices  30.1 us (36%)
  blocking collectives  12.7 us (15%)
  Pallas kernels  5.1 us (6%)
    all_to_all x1, waiting for transfers between devices, shards(): lax.all_to_all(ensemble_prediction[0], 'member', split_axis=0, concat_axi...  27.9 us
    all_to_all x1, starting transfers between devices, exchanged(): return lax.all_to_all(copies, axes, split_axis=0, concat_axis=0, tiled=True)  15.9 us
    all_to_all x1, blocking collectives, exchanged(): return lax.all_to_all(copies, axes, split_axis=0, concat_axis=0, tiled=True)  12.7 us
    all_to_all x1, starting transfers between devices, shards(): lax.all_to_all(ensemble_prediction[0], 'member', split_axis=0, concat_axi...  5.56 us
    all_to_all x1, waiting for transfers between devices, exchanged(): return lax.all_to_all(copies, axes, split_axis=0, concat_axis=0, tiled=True)  4.94 us
    ppermute x1, starting transfers between devices, add_up_and_send(): beside = lax.ppermute(codes, 'member', BESIDE)  3.64 us
    pallas_call x1, Pallas kernels, decode(): pl.pallas_call(decode_kernel, out_shape=(jax.ShapeDtypeStruct((VARIABLE_N...  3.34 us
    ppermute x1, starting transfers between devices, add_up_and_send(): corner = lax.ppermute(codes, 'member', CORNER)  3.1 us
  transfers between devices with their start and end apart: 5, of which 2 were waited for; matrix products, arithmetic and copies ran while one was open for 1% of the time, Pallas kernels for 0%

profile of v5, /device:TPU:1, one launch (start us, length us, event | category | flops | bytes accessed | tf_op | source)
XLA Modules:
  0.0 82.4 jit_solution(280568117385537145)
XLA Ops:
  0.6 0.0 copy-start.1
  0.6 0.0 copy-start
  0.6 5.6 %all-to-all-start.2 = ((bf16[300,16,128]{2,1,0:T(8,128)(2,1)}), bf16[300,16,128]{2,1,0:T(8,128)(2,1)S(1)}, u32[]{:S(2)}, u32[]{:S(2)}) async-start(bf16[300,16,128]{2,1,0:T(8,128)(2,1)} %bitcast.6), calls=%async_computation.2 | async-start | bytes 2457600 | tf_op jit(solution)/shard_map/all_to_all | solution.py:204
  6.2 0.1 fusion.6
  6.3 0.0 copy-done.1
  6.3 27.9 %all-to-all-done.2 = bf16[300,16,128]{2,1,0:T(8,128)(2,1)S(1)} async-done(((bf16[300,16,128]{2,1,0:T(8,128)(2,1)}), bf16[300,16,128]{2,1,0:T(8,128)(2,1)S(1)}, u32[]{:S(2)}, u32[]{:S(2)}) %all-to-all-start.2) | async-done | bytes 1228832 | tf_op jit(solution)/shard_map/all_to_all | solution.py:204
  34.2 0.0 copy-done
  34.2 1.8 %shard_map.50 = (s32[38,16,128]{2,1,0:T(8,128)S(1)}, f32[8,128]{1,0:T(8,128)S(1)}) custom-call(s32[1]{0:T(128)} %bitcast.1.member, bf16[4,75,16,128]{3,2,1,0:T(8,128)(2,1)S(1)} %bitcast.5, bf16[300,16,128]{2,1,0:T(8,128)(2,1)S(1)} %copy-done, f32[2,16,128]{2,1,0:T(8,128)S(1)} %compare_select_fusion.weight), custom_call_target="tpu_custom_call" | custom-call | flops 4608000 | bytes 2150400 | tf_op jit(solution)/shard_map/pallas_call | solution.py:79
  35.9 1.9 %collective-permute-start.2 = (s32[38,16,128]{2,1,0:T(8,128)S(1)}, s32[38,16,128]{2,1,0:T(8,128)S(1)}, u32[]{:S(2)}, u32[]{:S(2)}) collective-permute-start(s32[38,16,128]{2,1,0:T(8,128)S(1)} %get-tuple-element.27.own), channel_id=1, source_target_pairs={{0,256},{128,384},{256,0},{384,128},{1,257},{129,385},{257,1},{385... | collective-permute-start | bytes 933896 | tf_op jit(solution)/shard_map/ppermute | solution.py:219
  37.9 41.2 %conditional.2 = (s32[38,16,128]{2,1,0:T(8,128)}, s32[38,16,128]{2,1,0:T(8,128)}, f32[8,1,128]{2,1,0:T(1,128)}) conditional(s32[]{:T(128)} %convert_element_type.15, () %tuple.22, (s32[38,16,128]{2,1,0:T(8,128)S(1)}, pred[]{:T(512)}, f32[8,128]{1,0:T(8,128)S(1)}) %tuple.23), branch_computations={%region_0.1_spmd, %region_1.5_spmd} | conditional | flops 8065 | bytes 3193493 | solution.py:199
  37.9 0.8 broadcast_in_dim.9
  38.6 15.9 %all-to-all-start.1 = ((f32[320,1,128]{2,1,0:T(1,128)}), f32[320,1,128]{2,1,0:T(1,128)S(1)}, u32[]{:S(2)}, u32[]{:S(2)}) async-start(f32[320,1,128]{2,1,0:T(1,128)} %broadcast_in_dim.9), calls=%async_computation.1 | async-start | bytes 327680 | tf_op jit(solution)/shard_map/cond/branch_1_fun/all_to_all | solution.py:194
  54.6 3.1 %collective-permute-start.1 = (s32[38,16,128]{2,1,0:T(8,128)S(1)}, s32[38,16,128]{2,1,0:T(8,128)}, u32[]{:S(2)}, u32[]{:S(2)}) collective-permute-start(s32[38,16,128]{2,1,0:T(8,128)S(1)} %get-tuple-element.17), channel_id=1, source_target_pairs={{0,384},{128,256},{256,128},{384,0},{1,385},{129,257},{257,129},{3... | collective-permute-start | bytes 933896 | tf_op jit(solution)/shard_map/cond/branch_1_fun/ppermute | solution.py:223
  57.7 3.6 %collective-permute-start = (s32[38,16,128]{2,1,0:T(8,128)S(1)}, s32[38,16,128]{2,1,0:T(8,128)}, u32[]{:S(2)}, u32[]{:S(2)}) collective-permute-start(s32[38,16,128]{2,1,0:T(8,128)S(1)} %get-tuple-element.17), channel_id=1, source_target_pairs={{0,128},{128,0},{256,384},{384,256},{1,129},{129,1},{257,385},{385... | collective-permute-start | bytes 933896 | tf_op jit(solution)/shard_map/cond/branch_1_fun/ppermute | solution.py:222
  61.3 4.9 %all-to-all-done.1 = f32[320,1,128]{2,1,0:T(1,128)S(1)} async-done(((f32[320,1,128]{2,1,0:T(1,128)}), f32[320,1,128]{2,1,0:T(1,128)S(1)}, u32[]{:S(2)}, u32[]{:S(2)}) %all-to-all-start.1) | async-done | bytes 163872 | tf_op jit(solution)/shard_map/cond/branch_1_fun/all_to_all | solution.py:194
  66.3 12.8 %conditional = (f32[8,1,128]{2,1,0:T(1,128)}) conditional(s32[]{:T(128)} %convert_element_type.12, () %tuple.17, f32[320,1,128]{2,1,0:T(1,128)S(1)} %all-to-all-done.1), branch_computations={%region_2.2_spmd, %region_3.4_spmd} | conditional | flops 8064 | bytes 46088 | solution.py:199
  66.3 0.1 slice_reduce_fusion
  66.3 12.7 %all_to_all.14 = f32[8,1,128]{2,1,0:T(1,128)} all-to-all(f32[8,1,128]{2,1,0:T(1,128)S(1)} %broadcast_in_dim.3), channel_id=1, replica_groups=mesh['member'=4,'space_0'=8,'space_1'=2,'space_2'=4,'space_3'=2] {'membe..., dimensions={0} | all-to-all | bytes 8192 | tf_op jit(solution)/shard_map/cond/branch_1_fun/cond/branch_1_fun/all_to_all | solution.py:194
  79.0 0.0 collective-permute-done.1
  79.0 0.0 collective-permute-done
  79.0 0.0 collective-permute-done.2.across
  79.0 3.3 %shard_map.51 = (f32[300,16,128]{2,1,0:T(8,128)}, f32[300]{0:T(512)}) custom-call(s32[1]{0:T(128)} %bitcast.1.member, f32[8,1,128]{2,1,0:T(1,128)} %get-tuple-element.29.sums, s32[38,16,128]{2,1,0:T(8,128)S(1)} %get-tuple-element.27.own, s32[38,16,128]{2,1,0:T(8,128)S(1)} %collective-permute-done.2.across, s32[38,16,128]{2,1,0:T(8,128)} %get-tuple-element.30.beside, ...), custom_call_target="tpu_custom_call" | custom-call | flops 4980736 | bytes 3735552 | tf_op jit(solution)/shard_map/pallas_call | solution.py:165
  (3 shorter events, 0.0 us)
Async XLA Ops:
  0.6 5.7 %copy-start.1 = (s32[2,16,128]{2,1,0:T(8,128)S(1)}, s32[2,16,128]{2,1,0:T(8,128)}, u32[]{:S(2)}) copy-start(s32[2,16,128]{2,1,0:T(8,128)} %param.9) | copy-start | bytes 49156
  0.6 33.5 %copy-start = (bf16[300,16,128]{2,1,0:T(8,128)(2,1)S(1)}, bf16[300,16,128]{2,1,0:T(8,128)(2,1)}, u32[]{:S(2)}) copy-start(bf16[300,16,128]{2,1,0:T(8,128)(2,1)} %obs.1) | copy-start | bytes 3686404
  0.6 33.5 %all-to-all-start.2 = ((bf16[300,16,128]{2,1,0:T(8,128)(2,1)}), bf16[300,16,128]{2,1,0:T(8,128)(2,1)S(1)}, u32[]{:S(2)}, u32[]{:S(2)}) async-start(bf16[300,16,128]{2,1,0:T(8,128)(2,1)} %bitcast.6), calls=%async_computation.2 | async-start | bytes 2457600 | tf_op jit(solution)/shard_map/all_to_all | solution.py:204
  35.9 43.1 %collective-permute-start.2 = (s32[38,16,128]{2,1,0:T(8,128)S(1)}, s32[38,16,128]{2,1,0:T(8,128)S(1)}, u32[]{:S(2)}, u32[]{:S(2)}) collective-permute-start(s32[38,16,128]{2,1,0:T(8,128)S(1)} %get-tuple-element.27.own), channel_id=1, source_target_pairs={{0,256},{128,384},{256,0},{384,128},{1,257},{129,385},{257,1},{385... | collective-permute-start | bytes 933896 | tf_op jit(solution)/shard_map/ppermute | solution.py:219
  38.6 27.6 %all-to-all-start.1 = ((f32[320,1,128]{2,1,0:T(1,128)}), f32[320,1,128]{2,1,0:T(1,128)S(1)}, u32[]{:S(2)}, u32[]{:S(2)}) async-start(f32[320,1,128]{2,1,0:T(1,128)} %broadcast_in_dim.9), calls=%async_computation.1 | async-start | bytes 327680 | tf_op jit(solution)/shard_map/cond/branch_1_fun/all_to_all | solution.py:194
  54.6 24.5 %collective-permute-start.1 = (s32[38,16,128]{2,1,0:T(8,128)S(1)}, s32[38,16,128]{2,1,0:T(8,128)}, u32[]{:S(2)}, u32[]{:S(2)}) collective-permute-start(s32[38,16,128]{2,1,0:T(8,128)S(1)} %get-tuple-element.17), channel_id=1, source_target_pairs={{0,384},{128,256},{256,128},{384,0},{1,385},{129,257},{257,129},{3... | collective-permute-start | bytes 933896 | tf_op jit(solution)/shard_map/cond/branch_1_fun/ppermute | solution.py:223
  57.7 21.4 %collective-permute-start = (s32[38,16,128]{2,1,0:T(8,128)S(1)}, s32[38,16,128]{2,1,0:T(8,128)}, u32[]{:S(2)}, u32[]{:S(2)}) collective-permute-start(s32[38,16,128]{2,1,0:T(8,128)S(1)} %get-tuple-element.17), channel_id=1, source_target_pairs={{0,128},{128,0},{256,384},{384,256},{1,129},{129,1},{257,385},{385... | collective-permute-start | bytes 933896 | tf_op jit(solution)/shard_map/cond/branch_1_fun/ppermute | solution.py:222

commit v6 on v5

--- a/solution.py
+++ b/solution.py
@@ -14,31 +14,33 @@
 MEMBERS = 4
 SHARE = VARIABLE_NUMBER // MEMBERS
 SPACE = ("space_0", "space_1", "space_2", "space_3")
-ALONG_ZX = ("space_0", "space_2", "space_3")
-ALONG_Y = ("member", "space_1")
+ALONG_ZX = ("space_0", "space_2")
+ALONG_YC = ("member", "space_1", "space_3")
 COEFF = (1.0 - 0.05 / MEMBERS) / (2.0 * MEMBERS * (MEMBERS - 1))
 TOP = 32767.0
 BESIDE = [(m, m ^ 1) for m in range(MEMBERS)]
 ACROSS = [(m, m ^ 2) for m in range(MEMBERS)]
 CORNER = [(m, m ^ 3) for m in range(MEMBERS)]
-REPEATS = 5
+REPEATS = 10
 LEAST_EXPONENT = -120.0
 PAIRS = (SHARE + 1) // 2
 
 
-def encode_kernel(member, forecasts, obs, weight, codes, partial, values, rows):
+def encode_kernel(member, forecasts, obs, weight, codes, partial, values, rows, held, copied):
     first = member[0] * SHARE
 
     def score(i, top):
         target = obs[first + i].astype(jnp.float32)
-        a, b, c, d = (forecasts[m, i].astype(jnp.float32) for m in range(MEMBERS))
-        skill = jnp.abs(a - target) + jnp.abs(b - target) + jnp.abs(c - target) + jnp.abs(d - target)
+        a, b, c, d = (forecasts[m, i] for m in range(MEMBERS))
         low_ab, high_ab = jnp.minimum(a, b), jnp.maximum(a, b)
         low_cd, high_cd = jnp.minimum(c, d), jnp.maximum(c, d)
-        outer = jnp.maximum(high_ab, high_cd) - jnp.minimum(low_ab, low_cd)
-        inner = jnp.abs(jnp.minimum(high_ab, high_cd) - jnp.maximum(low_ab, low_cd))
+        least, most = jnp.minimum(low_ab, low_cd), jnp.maximum(high_ab, high_cd)
+        inner = jnp.minimum(high_ab, high_cd), jnp.maximum(low_ab, low_cd)
+        p, q, r, s = (x.astype(jnp.float32) for x in (least, most, *inner))
+        skill = jnp.abs(p - target) + jnp.abs(q - target) + jnp.abs(r - target) + jnp.abs(s - target)
+        spread = 3.0 * (q - p) + jnp.abs(r - s)
         group = (first + i >= ATMOS).astype(jnp.int32)
-        value = (skill * (1.0 / MEMBERS) - (2.0 * COEFF) * (3.0 * outer + inner)) * weight[group]
+        value = (skill * (1.0 / MEMBERS) - (2.0 * COEFF) * spread) * weight[group]
         values[i] = value
         rows[pl.ds(i, 1), :] = jnp.sum(value, axis=0, keepdims=True)
         return jnp.maximum(top, jnp.abs(value))
@@ -50,9 +52,12 @@
         valid = (weight[g] > 0.0).astype(jnp.float32)
         rows[SHARE + 2 + g : SHARE + 3 + g, :] = jnp.sum(valid, axis=0, keepdims=True)
     ones = jnp.ones((8, TILE_SITES), jnp.float32)
-    partial[...] = lax.dot_general(
+    sums = lax.dot_general(
         ones, rows[...], (((1,), (1,)), ((), ())), precision=lax.Precision.HIGHEST, preferred_element_type=jnp.float32
     )
+    held[...] = jnp.broadcast_to(sums[None, :1], held.shape)
+    copy = pltpu.make_async_copy(held, partial, copied)
+    copy.start()
 
     top = jnp.broadcast_to(jnp.max(top, keepdims=True), top.shape)
     k = jnp.where(top > 0.0, jnp.ceil(jnp.log2(jnp.where(top > 0.0, top, 1.0))), 0.0)
@@ -70,9 +75,10 @@
 
     lax.fori_loop(0, PAIRS - 1, pair, 0, unroll=4)
     codes[PAIRS - 1] = (k.astype(jnp.int32) << 16) | (code(values[PAIRS - 1]) & 0xFFFF)
-
-
-def encode(member, forecasts, obs, weight):
+    copy.wait()
+
+
+def encode(member, forecasts, obs, weight, number):
     blocks, sites = obs.shape[1:]
     share = (SHARE, blocks, sites)
     vmem = pl.BlockSpec(memory_space=pltpu.VMEM)
@@ -80,11 +86,16 @@
         encode_kernel,
         out_shape=(
             jax.ShapeDtypeStruct((PAIRS, blocks, sites), jnp.int32),
-            jax.ShapeDtypeStruct((8, sites), jnp.float32),
+            jax.ShapeDtypeStruct((number, 1, sites), jnp.float32),
         ),
         in_specs=[pl.BlockSpec(memory_space=pltpu.SMEM), vmem, vmem, vmem],
-        out_specs=(vmem, vmem),
-        scratch_shapes=[pltpu.VMEM(share, jnp.float32), pltpu.VMEM((sites, sites), jnp.float32)],
+        out_specs=(vmem, pl.BlockSpec(memory_space=pl.ANY)),
+        scratch_shapes=[
+            pltpu.VMEM(share, jnp.float32),
+            pltpu.VMEM((sites, sites), jnp.float32),
+            pltpu.VMEM((number, 1, sites), jnp.float32),
+            pltpu.SemaphoreType.DMA,
+        ],
         compiler_params=pltpu.CompilerParams(vmem_limit_bytes=24 << 20),
         cost_estimate=pl.CostEstimate(
             flops=30 * SHARE * blocks * sites, bytes_accessed=14 * SHARE * blocks * sites, transcendentals=0
@@ -214,7 +225,9 @@
     weight = (cosine * inside)[None] * (validity_flags > 0).astype(jnp.float32)
 
     member = lax.axis_index("member")[None]
-    codes, partial = encode(member, forecasts, observed_analysis, weight)
+    codes, partial = encode(
+        member, forecasts, observed_analysis, weight, REPEATS * lax.axis_size(ALONG_ZX)
+    )
     always = member[0] >= 0
     across = lax.ppermute(codes, "member", ACROSS)
 
@@ -222,12 +235,11 @@
         beside = lax.ppermute(codes, "member", BESIDE)
         corner = lax.ppermute(codes, "member", CORNER)
         over_zx = jnp.sum(exchanged(copies, ALONG_ZX)[::REPEATS], axis=0)
-        over_zx = copied(over_zx, lax.axis_size(ALONG_Y))
-        return beside, corner, in_one_step(always, lambda copies: exchanged(copies, ALONG_Y), over_zx)
-
-    copies = copied(partial[:1], REPEATS * lax.axis_size(ALONG_ZX))
-    beside, corner, over_y = in_one_step(always, add_up_and_send, codes, copies)
-    point_score, loss = decode(member, over_y, (codes, across, beside, corner))
+        over_zx = copied(over_zx, lax.axis_size(ALONG_YC))
+        return beside, corner, in_one_step(always, lambda copies: exchanged(copies, ALONG_YC), over_zx)
+
+    beside, corner, over_yc = in_one_step(always, add_up_and_send, codes, partial)
+    point_score, loss = decode(member, over_yc, (codes, across, beside, corner))
     return (point_score, loss)
 
 

time: 82.8 us -> 82.1 us (level)
  blocking collectives: 12.7 us -> 16.5 us
  starting transfers between devices: 30.1 us -> 28 us
  waiting for transfers between devices: 32.8 us -> 31 us
    all_to_all x1, blocking collectives: 12.7 us -> 16.5 us  [exchanged(): return lax.all_to_all(copies, axes, split_axis=0, concat_axis=0, tiled=True)]
    all_to_all x1, starting transfers between devices: 15.9 us -> 14 us  [exchanged(): return lax.all_to_all(copies, axes, split_axis=0, concat_axis=0, tiled=True)]
    all_to_all x1, waiting for transfers between devices: 4.94 us -> 3.14 us  [exchanged(): return lax.all_to_all(copies, axes, split_axis=0, concat_axis=0, tiled=True)]
  transfers between devices with their start and end apart: 5 -> 5, of which waited for: 2 -> 2; matrix products, arithmetic and copies ran while one was open for 1% -> 0% of each run, Pallas kernels for 0% -> 0%
where the time goes in v6:
time: 82.1 us; the launch traced here: 81.7 us
  waiting for transfers between devices  31 us (38%)
  starting transfers between devices  28 us (34%)
  blocking collectives  16.5 us (20%)
  Pallas kernels  5.31 us (6%)
    all_to_all x1, waiting for transfers between devices, shards(): lax.all_to_all(ensemble_prediction[0], 'member', split_axis=0, concat_axi...  27.9 us
    all_to_all x1, blocking collectives, exchanged(): return lax.all_to_all(copies, axes, split_axis=0, concat_axis=0, tiled=True)  16.5 us
    all_to_all x1, starting transfers between devices, exchanged(): return lax.all_to_all(copies, axes, split_axis=0, concat_axis=0, tiled=True)  14 us
    all_to_all x1, starting transfers between devices, shards(): lax.all_to_all(ensemble_prediction[0], 'member', split_axis=0, concat_axi...  5.56 us
    ppermute x1, starting transfers between devices, add_up_and_send(): beside = lax.ppermute(codes, 'member', BESIDE)  3.78 us
    pallas_call x1, Pallas kernels, decode(): pl.pallas_call(decode_kernel, out_shape=(jax.ShapeDtypeStruct((VARIABLE_N...  3.36 us
    all_to_all x1, waiting for transfers between devices, exchanged(): return lax.all_to_all(copies, axes, split_axis=0, concat_axis=0, tiled=True)  3.14 us
    ppermute x1, starting transfers between devices, add_up_and_send(): corner = lax.ppermute(codes, 'member', CORNER)  2.67 us
  transfers between devices with their start and end apart: 5, of which 2 were waited for; matrix products, arithmetic and copies ran while one was open for 0% of the time, Pallas kernels for 0%

profile of v6, /device:TPU:1, one launch (start us, length us, event | category | flops | bytes accessed | tf_op | source)
XLA Modules:
  0.0 81.7 jit_solution(17472877287043082711)
XLA Ops:
  0.6 0.0 copy-start.1
  0.6 0.0 copy-start
  0.6 5.6 %all-to-all-start.2 = ((bf16[300,16,128]{2,1,0:T(8,128)(2,1)}), bf16[300,16,128]{2,1,0:T(8,128)(2,1)S(1)}, u32[]{:S(2)}, u32[]{:S(2)}) async-start(bf16[300,16,128]{2,1,0:T(8,128)(2,1)} %bitcast.4), calls=%async_computation.2 | async-start | bytes 2457600 | tf_op jit(solution)/shard_map/all_to_all | solution.py:215
  6.2 0.1 fusion.6
  6.3 0.0 copy-done.1
  6.3 27.9 %all-to-all-done.2 = bf16[300,16,128]{2,1,0:T(8,128)(2,1)S(1)} async-done(((bf16[300,16,128]{2,1,0:T(8,128)(2,1)}), bf16[300,16,128]{2,1,0:T(8,128)(2,1)S(1)}, u32[]{:S(2)}, u32[]{:S(2)}) %all-to-all-start.2) | async-done | bytes 1228832 | tf_op jit(solution)/shard_map/all_to_all | solution.py:215
  34.2 0.0 copy-done
  34.2 1.9 %shard_map.50 = (s32[38,16,128]{2,1,0:T(8,128)S(1)}, f32[320,1,128]{2,1,0:T(1,128)}) custom-call(s32[1]{0:T(128)} %bitcast.member, bf16[4,75,16,128]{3,2,1,0:T(8,128)(2,1)S(1)} %bitcast.3, bf16[300,16,128]{2,1,0:T(8,128)(2,1)S(1)} %copy-done, f32[2,16,128]{2,1,0:T(8,128)S(1)} %compare_select_fusion.weight), custom_call_target="tpu_custom_call" | custom-call | flops 4608000 | bytes 2150400 | tf_op jit(solution)/shard_map/pallas_call | solution.py:85
  36.1 1.9 %collective-permute-start.2 = (s32[38,16,128]{2,1,0:T(8,128)S(1)}, s32[38,16,128]{2,1,0:T(8,128)S(1)}, u32[]{:S(2)}, u32[]{:S(2)}) collective-permute-start(s32[38,16,128]{2,1,0:T(8,128)S(1)} %get-tuple-element.24.own), channel_id=1, source_target_pairs={{0,256},{128,384},{256,0},{384,128},{1,257},{129,385},{257,1},{385... | collective-permute-start | bytes 933896 | tf_op jit(solution)/shard_map/ppermute | solution.py:232
  38.0 40.2 %conditional.2 = (s32[38,16,128]{2,1,0:T(8,128)}, s32[38,16,128]{2,1,0:T(8,128)}, f32[16,1,128]{2,1,0:T(1,128)}) conditional(s32[]{:T(128)} %convert_element_type.15, () %tuple.22, (s32[38,16,128]{2,1,0:T(8,128)S(1)}, pred[]{:T(512)}, f32[320,1,128]{2,1,0:T(1,128)}) %tuple.23), branch_computations={%region_0.1_spmd, %region_1.5_spmd} | conditional | flops 3969 | bytes 3024021 | solution.py:210
  38.1 14.0 %all-to-all-start.1 = ((f32[320,1,128]{2,1,0:T(1,128)}), f32[320,1,128]{2,1,0:T(1,128)S(1)}, u32[]{:S(2)}, u32[]{:S(2)}) async-start(f32[320,1,128]{2,1,0:T(1,128)} %get-tuple-element.16), calls=%async_computation.1 | async-start | bytes 327680 | tf_op jit(solution)/shard_map/cond/branch_1_fun/all_to_all | solution.py:205
  52.1 2.7 %collective-permute-start.1 = (s32[38,16,128]{2,1,0:T(8,128)S(1)}, s32[38,16,128]{2,1,0:T(8,128)}, u32[]{:S(2)}, u32[]{:S(2)}) collective-permute-start(s32[38,16,128]{2,1,0:T(8,128)S(1)} %get-tuple-element.14), channel_id=1, source_target_pairs={{0,384},{128,256},{256,128},{384,0},{1,385},{129,257},{257,129},{3... | collective-permute-start | bytes 933896 | tf_op jit(solution)/shard_map/cond/branch_1_fun/ppermute | solution.py:236
  54.8 3.8 %collective-permute-start = (s32[38,16,128]{2,1,0:T(8,128)S(1)}, s32[38,16,128]{2,1,0:T(8,128)}, u32[]{:S(2)}, u32[]{:S(2)}) collective-permute-start(s32[38,16,128]{2,1,0:T(8,128)S(1)} %get-tuple-element.14), channel_id=1, source_target_pairs={{0,128},{128,0},{256,384},{384,256},{1,129},{129,1},{257,385},{385... | collective-permute-start | bytes 933896 | tf_op jit(solution)/shard_map/cond/branch_1_fun/ppermute | solution.py:235
  58.6 3.1 %all-to-all-done.1 = f32[320,1,128]{2,1,0:T(1,128)S(1)} async-done(((f32[320,1,128]{2,1,0:T(1,128)}), f32[320,1,128]{2,1,0:T(1,128)S(1)}, u32[]{:S(2)}, u32[]{:S(2)}) %all-to-all-start.1) | async-done | bytes 163872 | tf_op jit(solution)/shard_map/cond/branch_1_fun/all_to_all | solution.py:205
  61.7 16.6 %conditional = (f32[16,1,128]{2,1,0:T(1,128)}) conditional(s32[]{:T(128)} %convert_element_type.12, () %tuple.17, f32[320,1,128]{2,1,0:T(1,128)S(1)} %all-to-all-done.1), branch_computations={%region_2.2_spmd, %region_3.4_spmd} | conditional | flops 3968 | bytes 41992 | solution.py:210
  61.8 16.5 %all_to_all.14 = f32[16,1,128]{2,1,0:T(1,128)} all-to-all(f32[16,1,128]{2,1,0:T(1,128)S(1)} %broadcast_in_dim.4), channel_id=1, replica_groups=mesh['member'=4,'space_0'=8,'space_1'=2,'space_2'=4,'space_3'=2] {'membe..., dimensions={0} | all-to-all | bytes 16384 | tf_op jit(solution)/shard_map/cond/branch_1_fun/cond/branch_1_fun/all_to_all | solution.py:205
  78.3 0.0 collective-permute-done.1
  78.3 0.0 collective-permute-done
  78.3 0.0 collective-permute-done.2.across
  78.3 3.4 %shard_map.51 = (f32[300,16,128]{2,1,0:T(8,128)}, f32[300]{0:T(512)}) custom-call(s32[1]{0:T(128)} %bitcast.member, f32[16,1,128]{2,1,0:T(1,128)} %get-tuple-element.26.sums, s32[38,16,128]{2,1,0:T(8,128)S(1)} %get-tuple-element.24.own, s32[38,16,128]{2,1,0:T(8,128)S(1)} %collective-permute-done.2.across, s32[38,16,128]{2,1,0:T(8,128)} %get-tuple-element.27.beside, ...), custom_call_target="tpu_custom_call" | custom-call | flops 4980736 | bytes 3735552 | tf_op jit(solution)/shard_map/pallas_call | solution.py:176
  (3 shorter events, 0.1 us)
Async XLA Ops:
  0.6 5.7 %copy-start.1 = (s32[2,16,128]{2,1,0:T(8,128)S(1)}, s32[2,16,128]{2,1,0:T(8,128)}, u32[]{:S(2)}) copy-start(s32[2,16,128]{2,1,0:T(8,128)} %param.9) | copy-start | bytes 49156
  0.6 33.5 %copy-start = (bf16[300,16,128]{2,1,0:T(8,128)(2,1)S(1)}, bf16[300,16,128]{2,1,0:T(8,128)(2,1)}, u32[]{:S(2)}) copy-start(bf16[300,16,128]{2,1,0:T(8,128)(2,1)} %obs.1) | copy-start | bytes 3686404
  0.6 33.5 %all-to-all-start.2 = ((bf16[300,16,128]{2,1,0:T(8,128)(2,1)}), bf16[300,16,128]{2,1,0:T(8,128)(2,1)S(1)}, u32[]{:S(2)}, u32[]{:S(2)}) async-start(bf16[300,16,128]{2,1,0:T(8,128)(2,1)} %bitcast.4), calls=%async_computation.2 | async-start | bytes 2457600 | tf_op jit(solution)/shard_map/all_to_all | solution.py:215
  36.1 42.2 %collective-permute-start.2 = (s32[38,16,128]{2,1,0:T(8,128)S(1)}, s32[38,16,128]{2,1,0:T(8,128)S(1)}, u32[]{:S(2)}, u32[]{:S(2)}) collective-permute-start(s32[38,16,128]{2,1,0:T(8,128)S(1)} %get-tuple-element.24.own), channel_id=1, source_target_pairs={{0,256},{128,384},{256,0},{384,128},{1,257},{129,385},{257,1},{385... | collective-permute-start | bytes 933896 | tf_op jit(solution)/shard_map/ppermute | solution.py:232
  38.1 23.7 %all-to-all-start.1 = ((f32[320,1,128]{2,1,0:T(1,128)}), f32[320,1,128]{2,1,0:T(1,128)S(1)}, u32[]{:S(2)}, u32[]{:S(2)}) async-start(f32[320,1,128]{2,1,0:T(1,128)} %get-tuple-element.16), calls=%async_computation.1 | async-start | bytes 327680 | tf_op jit(solution)/shard_map/cond/branch_1_fun/all_to_all | solution.py:205
  52.1 26.2 %collective-permute-start.1 = (s32[38,16,128]{2,1,0:T(8,128)S(1)}, s32[38,16,128]{2,1,0:T(8,128)}, u32[]{:S(2)}, u32[]{:S(2)}) collective-permute-start(s32[38,16,128]{2,1,0:T(8,128)S(1)} %get-tuple-element.14), channel_id=1, source_target_pairs={{0,384},{128,256},{256,128},{384,0},{1,385},{129,257},{257,129},{3... | collective-permute-start | bytes 933896 | tf_op jit(solution)/shard_map/cond/branch_1_fun/ppermute | solution.py:236
  54.8 23.5 %collective-permute-start = (s32[38,16,128]{2,1,0:T(8,128)S(1)}, s32[38,16,128]{2,1,0:T(8,128)}, u32[]{:S(2)}, u32[]{:S(2)}) collective-permute-start(s32[38,16,128]{2,1,0:T(8,128)S(1)} %get-tuple-element.14), channel_id=1, source_target_pairs={{0,128},{128,0},{256,384},{384,256},{1,129},{129,1},{257,385},{385... | collective-permute-start | bytes 933896 | tf_op jit(solution)/shard_map/cond/branch_1_fun/ppermute | solution.py:235

commit v7 on v6

--- a/solution.py
+++ b/solution.py
@@ -103,93 +103,82 @@
     )(member, forecasts, obs, weight)
 
 
-def in_order(step):
-    return (step & 1) * 2 + (step >> 1)
-
-
-def decode_kernel(member, sums, own, across, beside, corner, out, loss, scale, units, held, copied):
-    step = pl.program_id(0)
+def decode_kernel(member, sums_here, own, across, beside, corner, out, loss, sums, scores, held, arrived, left):
+    come = [
+        pltpu.make_async_copy(here, there, arrived.at[n])
+        for n, (here, there) in enumerate(((sums_here, sums), (beside, held.at[0]), (corner, held.at[1])))
+    ]
+    for copy in come:
+        copy.start()
+    come[0].wait()
     halves = sums.shape[0] // MEMBERS
-    copies = [pltpu.make_async_copy(codes, held.at[s], copied.at[s]) for s, codes in enumerate((beside, corner))]
-
-    def total(m):
-        return sum(sums[m * halves + h] for h in range(halves))
+    totals = [sum(sums[m * halves + h] for h in range(halves)) for m in range(MEMBERS)]
+    lane = lax.broadcasted_iota(jnp.int32, totals[0].shape, 1)
 
     def at(i):
-        row = total(0)
-        lane = lax.broadcasted_iota(jnp.int32, row.shape, 1)
-        return jnp.sum(jnp.where(lane == i, row, 0.0), keepdims=True)
-
-    @pl.when(step == 0)
-    def _():
-        for copy in copies:
-            copy.start()
-        for g in range(2):
-            scale[g] = jnp.broadcast_to(at(SHARE + 2 + g) / at(SHARE + g), scale.shape[1:])
-
-    @pl.when(step == 1)
-    def _():
-        width = 3 * TILE_SITES
-        channel = lax.broadcasted_iota(jnp.int32, (1, width), 1)
-        wide = jnp.zeros((1, width), jnp.float32)
-        blank = jnp.zeros((1, width - TILE_SITES), jnp.float32)
-        for m in range(MEMBERS):
-            moved = pltpu.roll(jnp.concatenate([total(m), blank], axis=1), m * SHARE, 1)
-            wide = jnp.where((channel >= m * SHARE) & (channel < (m + 1) * SHARE), moved, wide)
-        wide = wide / jnp.where(channel >= ATMOS, at(SHARE + 1), at(SHARE))
-        loss[...] = wide[0, :VARIABLE_NUMBER]
-
-    first = (member[0] ^ in_order(step)) * SHARE
-
-    def share(codes):
+        return jnp.sum(jnp.where(lane == i, totals[0], 0.0), keepdims=True)
+
+    area = [at(SHARE + g) for g in range(2)]
+    scale = [jnp.broadcast_to(at(SHARE + 2 + g) / area[g], own.shape[1:]) for g in range(2)]
+
+    go = []
+    for n, (partner, codes) in enumerate(((0, own), (2, across), (1, held.at[0]), (3, held.at[1]))):
+        if n >= 2:
+            come[n - 1].wait()
+        first = (member[0] ^ partner) * SHARE
         unit = jnp.exp2((codes[PAIRS - 1] >> 16).astype(jnp.float32)) * (1.0 / TOP**4)
-        for g in range(2):
-            units[g] = unit * scale[g]
-
-        def write(i, code):
+        units = [unit * scale[g] for g in range(2)]
+
+        def write(i, code, n=n, first=first, units=units):
             steps = code.astype(jnp.float32)
             square = steps * steps
-            group = (first + i >= ATMOS).astype(jnp.int32)
-            out[i] = (steps * jnp.abs(steps)) * square * units[group]
-
-        def pair(i, carry):
+            unit = jnp.where(first + i >= ATMOS, units[1], units[0])
+            scores[n, i] = (steps * jnp.abs(steps)) * square * unit
+
+        def pair(i, carry, codes=codes, write=write):
             both = codes[i]
             write(i, (both << 16) >> 16)
             write(PAIRS + i, both >> 16)
             return carry
 
-        lax.fori_loop(0, PAIRS - 1, pair, 0, unroll=4)
+        lax.fori_loop(0, PAIRS - 1, pair, 0, unroll=True)
         write(PAIRS - 1, (codes[PAIRS - 1] << 16) >> 16)
-
-    for s, codes in enumerate((own, across, held.at[0], held.at[1])):
-
-        @pl.when(step == s)
-        def _(s=s, codes=codes):
-            if s >= 2:
-                copies[s - 2].wait()
-            share(codes)
+        copy = pltpu.make_async_copy(scores.at[n], out.at[pl.ds(first, SHARE)], left.at[n])
+        copy.start()
+        go.append(copy)
+
+    width = 3 * TILE_SITES
+    channel = lax.broadcasted_iota(jnp.int32, (1, width), 1)
+    wide = jnp.zeros((1, width), jnp.float32)
+    blank = jnp.zeros((1, width - TILE_SITES), jnp.float32)
+    for m in range(MEMBERS):
+        moved = pltpu.roll(jnp.concatenate([totals[m], blank], axis=1), m * SHARE, 1)
+        wide = jnp.where((channel >= m * SHARE) & (channel < (m + 1) * SHARE), moved, wide)
+    wide = wide / jnp.where(channel >= ATMOS, area[1], area[0])
+    loss[...] = wide[0, :VARIABLE_NUMBER]
+    for copy in go:
+        copy.wait()
 
 
 def decode(member, sums, shares):
     blocks, sites = shares[0].shape[1:]
     vmem = pl.BlockSpec(memory_space=pltpu.VMEM)
+    anywhere = pl.BlockSpec(memory_space=pl.ANY)
     return pl.pallas_call(
         decode_kernel,
         out_shape=(
             jax.ShapeDtypeStruct((VARIABLE_NUMBER, blocks, sites), jnp.float32),
             jax.ShapeDtypeStruct((VARIABLE_NUMBER,), jnp.float32),
         ),
-        grid_spec=pltpu.PrefetchScalarGridSpec(
-            num_scalar_prefetch=1,
-            grid=(MEMBERS,),
-            in_specs=[vmem] * 3 + [pl.BlockSpec(memory_space=pl.ANY)] * 2,
-            out_specs=(
-                pl.BlockSpec((SHARE, blocks, sites), lambda s, member: (member[0] ^ in_order(s), 0, 0)),
-                pl.BlockSpec((VARIABLE_NUMBER,), lambda s, member: (0,)),
-            ),
-            scratch_shapes=[pltpu.VMEM((2, blocks, sites), jnp.float32)] * 2
-            + [pltpu.VMEM((2, *shares[0].shape), jnp.int32), pltpu.SemaphoreType.DMA((2,))],
-        ),
+        in_specs=[pl.BlockSpec(memory_space=pltpu.SMEM), anywhere, vmem, vmem, anywhere, anywhere],
+        out_specs=(anywhere, vmem),
+        scratch_shapes=[
+            pltpu.VMEM(sums.shape, jnp.float32),
+            pltpu.VMEM((MEMBERS, SHARE, blocks, sites), jnp.float32),
+            pltpu.VMEM((2, *shares[0].shape), jnp.int32),
+            pltpu.SemaphoreType.DMA((3,)),
+            pltpu.SemaphoreType.DMA((MEMBERS,)),
+        ],
         compiler_params=pltpu.CompilerParams(vmem_limit_bytes=24 << 20),
         cost_estimate=pl.CostEstimate(
             flops=64 * shares[0].size, bytes_accessed=48 * shares[0].size, transcendentals=0

time: 82.1 us -> 81.7 us (level)
  no operation moved by 1% of the time
where the time goes in v7:
time: 81.7 us; the launch traced here: 81.3 us
  waiting for transfers between devices  31 us (38%)
  starting transfers between devices  28 us (34%)
  blocking collectives  16.5 us (20%)
  Pallas kernels  4.95 us (6%)
    all_to_all x1, waiting for transfers between devices, shards(): lax.all_to_all(ensemble_prediction[0], 'member', split_axis=0, concat_axi...  27.9 us
    all_to_all x1, blocking collectives, exchanged(): return lax.all_to_all(copies, axes, split_axis=0, concat_axis=0, tiled=True)  16.5 us
    all_to_all x1, starting transfers between devices, exchanged(): return lax.all_to_all(copies, axes, split_axis=0, concat_axis=0, tiled=True)  14 us
    all_to_all x1, starting transfers between devices, shards(): lax.all_to_all(ensemble_prediction[0], 'member', split_axis=0, concat_axi...  5.56 us
    ppermute x1, starting transfers between devices, add_up_and_send(): beside = lax.ppermute(codes, 'member', BESIDE)  3.78 us
    all_to_all x1, waiting for transfers between devices, exchanged(): return lax.all_to_all(copies, axes, split_axis=0, concat_axis=0, tiled=True)  3.14 us
    pallas_call x1, Pallas kernels, decode(): pl.pallas_call(decode_kernel, out_shape=(jax.ShapeDtypeStruct((VARIABLE_N...  3.01 us
    ppermute x1, starting transfers between devices, add_up_and_send(): corner = lax.ppermute(codes, 'member', CORNER)  2.67 us
  transfers between devices with their start and end apart: 5, of which 2 were waited for; matrix products, arithmetic and copies ran while one was open for 0% of the time, Pallas kernels for 0%

profile of v7, /device:TPU:1, one launch (start us, length us, event | category | flops | bytes accessed | tf_op | source)
XLA Modules:
  0.0 81.3 jit_solution(484701117524566003)
XLA Ops:
  0.6 0.0 copy-start.1
  0.6 0.0 copy-start
  0.6 5.6 %all-to-all-start.2 = ((bf16[300,16,128]{2,1,0:T(8,128)(2,1)}), bf16[300,16,128]{2,1,0:T(8,128)(2,1)S(1)}, u32[]{:S(2)}, u32[]{:S(2)}) async-start(bf16[300,16,128]{2,1,0:T(8,128)(2,1)} %bitcast.4), calls=%async_computation.2 | async-start | bytes 2457600 | tf_op jit(solution)/shard_map/all_to_all | solution.py:204
  6.2 0.1 fusion.6
  6.3 0.0 copy-done.1
  6.3 27.9 %all-to-all-done.2 = bf16[300,16,128]{2,1,0:T(8,128)(2,1)S(1)} async-done(((bf16[300,16,128]{2,1,0:T(8,128)(2,1)}), bf16[300,16,128]{2,1,0:T(8,128)(2,1)S(1)}, u32[]{:S(2)}, u32[]{:S(2)}) %all-to-all-start.2) | async-done | bytes 1228832 | tf_op jit(solution)/shard_map/all_to_all | solution.py:204
  34.2 0.0 copy-done
  34.2 1.9 %shard_map.50 = (s32[38,16,128]{2,1,0:T(8,128)S(1)}, f32[320,1,128]{2,1,0:T(1,128)}) custom-call(s32[1]{0:T(128)} %bitcast.member, bf16[4,75,16,128]{3,2,1,0:T(8,128)(2,1)S(1)} %bitcast.3, bf16[300,16,128]{2,1,0:T(8,128)(2,1)S(1)} %copy-done, f32[2,16,128]{2,1,0:T(8,128)S(1)} %compare_select_fusion.weight), custom_call_target="tpu_custom_call" | custom-call | flops 4608000 | bytes 2150400 | tf_op jit(solution)/shard_map/pallas_call | solution.py:85
  36.1 1.9 %collective-permute-start.2 = (s32[38,16,128]{2,1,0:T(8,128)S(1)}, s32[38,16,128]{2,1,0:T(8,128)S(1)}, u32[]{:S(2)}, u32[]{:S(2)}) collective-permute-start(s32[38,16,128]{2,1,0:T(8,128)S(1)} %get-tuple-element.24.own), channel_id=1, source_target_pairs={{0,256},{128,384},{256,0},{384,128},{1,257},{129,385},{257,1},{385... | collective-permute-start | bytes 933896 | tf_op jit(solution)/shard_map/ppermute | solution.py:221
  38.0 40.2 %conditional.2 = (s32[38,16,128]{2,1,0:T(8,128)}, s32[38,16,128]{2,1,0:T(8,128)}, f32[16,1,128]{2,1,0:T(1,128)}) conditional(s32[]{:T(128)} %convert_element_type.15, () %tuple.22, (s32[38,16,128]{2,1,0:T(8,128)S(1)}, pred[]{:T(512)}, f32[320,1,128]{2,1,0:T(1,128)}) %tuple.23), branch_computations={%region_0.1_spmd, %region_1.5_spmd} | conditional | flops 3969 | bytes 3024021 | solution.py:199
  38.1 14.0 %all-to-all-start.1 = ((f32[320,1,128]{2,1,0:T(1,128)}), f32[320,1,128]{2,1,0:T(1,128)S(1)}, u32[]{:S(2)}, u32[]{:S(2)}) async-start(f32[320,1,128]{2,1,0:T(1,128)} %get-tuple-element.16), calls=%async_computation.1 | async-start | bytes 327680 | tf_op jit(solution)/shard_map/cond/branch_1_fun/all_to_all | solution.py:194
  52.1 2.7 %collective-permute-start.1 = (s32[38,16,128]{2,1,0:T(8,128)S(1)}, s32[38,16,128]{2,1,0:T(8,128)}, u32[]{:S(2)}, u32[]{:S(2)}) collective-permute-start(s32[38,16,128]{2,1,0:T(8,128)S(1)} %get-tuple-element.14), channel_id=1, source_target_pairs={{0,384},{128,256},{256,128},{384,0},{1,385},{129,257},{257,129},{3... | collective-permute-start | bytes 933896 | tf_op jit(solution)/shard_map/cond/branch_1_fun/ppermute | solution.py:225
  54.8 3.8 %collective-permute-start = (s32[38,16,128]{2,1,0:T(8,128)S(1)}, s32[38,16,128]{2,1,0:T(8,128)}, u32[]{:S(2)}, u32[]{:S(2)}) collective-permute-start(s32[38,16,128]{2,1,0:T(8,128)S(1)} %get-tuple-element.14), channel_id=1, source_target_pairs={{0,128},{128,0},{256,384},{384,256},{1,129},{129,1},{257,385},{385... | collective-permute-start | bytes 933896 | tf_op jit(solution)/shard_map/cond/branch_1_fun/ppermute | solution.py:224
  58.6 3.1 %all-to-all-done.1 = f32[320,1,128]{2,1,0:T(1,128)S(1)} async-done(((f32[320,1,128]{2,1,0:T(1,128)}), f32[320,1,128]{2,1,0:T(1,128)S(1)}, u32[]{:S(2)}, u32[]{:S(2)}) %all-to-all-start.1) | async-done | bytes 163872 | tf_op jit(solution)/shard_map/cond/branch_1_fun/all_to_all | solution.py:194
  61.7 16.6 %conditional = (f32[16,1,128]{2,1,0:T(1,128)}) conditional(s32[]{:T(128)} %convert_element_type.12, () %tuple.17, f32[320,1,128]{2,1,0:T(1,128)S(1)} %all-to-all-done.1), branch_computations={%region_2.2_spmd, %region_3.4_spmd} | conditional | flops 3968 | bytes 41992 | solution.py:199
  61.8 16.5 %all_to_all.14 = f32[16,1,128]{2,1,0:T(1,128)} all-to-all(f32[16,1,128]{2,1,0:T(1,128)S(1)} %broadcast_in_dim.4), channel_id=1, replica_groups=mesh['member'=4,'space_0'=8,'space_1'=2,'space_2'=4,'space_3'=2] {'membe..., dimensions={0} | all-to-all | bytes 16384 | tf_op jit(solution)/shard_map/cond/branch_1_fun/cond/branch_1_fun/all_to_all | solution.py:194
  78.3 0.0 collective-permute-done.1
  78.3 0.0 collective-permute-done
  78.3 0.0 collective-permute-done.2.across
  78.3 3.0 %shard_map.51 = (f32[300,16,128]{2,1,0:T(8,128)}, f32[300]{0:T(512)}) custom-call(s32[1]{0:T(128)} %bitcast.member, f32[16,1,128]{2,1,0:T(1,128)} %get-tuple-element.26.sums_here, s32[38,16,128]{2,1,0:T(8,128)S(1)} %get-tuple-element.24.own, s32[38,16,128]{2,1,0:T(8,128)S(1)} %collective-permute-done.2.across, s32[38,16,128]{2,1,0:T(8,128)} %get-tuple-element.27.beside, ...), custom_call_target="tpu_custom_call" | custom-call | flops 4980736 | bytes 3735552 | tf_op jit(solution)/shard_map/pallas_call | solution.py:167
  (3 shorter events, 0.1 us)
Async XLA Ops:
  0.6 5.7 %copy-start.1 = (s32[2,16,128]{2,1,0:T(8,128)S(1)}, s32[2,16,128]{2,1,0:T(8,128)}, u32[]{:S(2)}) copy-start(s32[2,16,128]{2,1,0:T(8,128)} %param.9) | copy-start | bytes 49156
  0.6 33.5 %copy-start = (bf16[300,16,128]{2,1,0:T(8,128)(2,1)S(1)}, bf16[300,16,128]{2,1,0:T(8,128)(2,1)}, u32[]{:S(2)}) copy-start(bf16[300,16,128]{2,1,0:T(8,128)(2,1)} %obs.1) | copy-start | bytes 3686404
  0.6 33.5 %all-to-all-start.2 = ((bf16[300,16,128]{2,1,0:T(8,128)(2,1)}), bf16[300,16,128]{2,1,0:T(8,128)(2,1)S(1)}, u32[]{:S(2)}, u32[]{:S(2)}) async-start(bf16[300,16,128]{2,1,0:T(8,128)(2,1)} %bitcast.4), calls=%async_computation.2 | async-start | bytes 2457600 | tf_op jit(solution)/shard_map/all_to_all | solution.py:204
  36.1 42.2 %collective-permute-start.2 = (s32[38,16,128]{2,1,0:T(8,128)S(1)}, s32[38,16,128]{2,1,0:T(8,128)S(1)}, u32[]{:S(2)}, u32[]{:S(2)}) collective-permute-start(s32[38,16,128]{2,1,0:T(8,128)S(1)} %get-tuple-element.24.own), channel_id=1, source_target_pairs={{0,256},{128,384},{256,0},{384,128},{1,257},{129,385},{257,1},{385... | collective-permute-start | bytes 933896 | tf_op jit(solution)/shard_map/ppermute | solution.py:221
  38.1 23.7 %all-to-all-start.1 = ((f32[320,1,128]{2,1,0:T(1,128)}), f32[320,1,128]{2,1,0:T(1,128)S(1)}, u32[]{:S(2)}, u32[]{:S(2)}) async-start(f32[320,1,128]{2,1,0:T(1,128)} %get-tuple-element.16), calls=%async_computation.1 | async-start | bytes 327680 | tf_op jit(solution)/shard_map/cond/branch_1_fun/all_to_all | solution.py:194
  52.1 26.2 %collective-permute-start.1 = (s32[38,16,128]{2,1,0:T(8,128)S(1)}, s32[38,16,128]{2,1,0:T(8,128)}, u32[]{:S(2)}, u32[]{:S(2)}) collective-permute-start(s32[38,16,128]{2,1,0:T(8,128)S(1)} %get-tuple-element.14), channel_id=1, source_target_pairs={{0,384},{128,256},{256,128},{384,0},{1,385},{129,257},{257,129},{3... | collective-permute-start | bytes 933896 | tf_op jit(solution)/shard_map/cond/branch_1_fun/ppermute | solution.py:225
  54.8 23.5 %collective-permute-start = (s32[38,16,128]{2,1,0:T(8,128)S(1)}, s32[38,16,128]{2,1,0:T(8,128)}, u32[]{:S(2)}, u32[]{:S(2)}) collective-permute-start(s32[38,16,128]{2,1,0:T(8,128)S(1)} %get-tuple-element.14), channel_id=1, source_target_pairs={{0,128},{128,0},{256,384},{384,256},{1,129},{129,1},{257,385},{385... | collective-permute-start | bytes 933896 | tf_op jit(solution)/shard_map/cond/branch_1_fun/ppermute | solution.py:224

commit v8 on v7

--- a/solution.py
+++ b/solution.py
@@ -31,14 +31,13 @@
 
     def score(i, top):
         target = obs[first + i].astype(jnp.float32)
-        a, b, c, d = (forecasts[m, i] for m in range(MEMBERS))
+        a, b, c, d = (forecasts[m, i].astype(jnp.float32) for m in range(MEMBERS))
+        skill = jnp.abs(a - target) + jnp.abs(b - target) + jnp.abs(c - target) + jnp.abs(d - target)
         low_ab, high_ab = jnp.minimum(a, b), jnp.maximum(a, b)
         low_cd, high_cd = jnp.minimum(c, d), jnp.maximum(c, d)
-        least, most = jnp.minimum(low_ab, low_cd), jnp.maximum(high_ab, high_cd)
-        inner = jnp.minimum(high_ab, high_cd), jnp.maximum(low_ab, low_cd)
-        p, q, r, s = (x.astype(jnp.float32) for x in (least, most, *inner))
-        skill = jnp.abs(p - target) + jnp.abs(q - target) + jnp.abs(r - target) + jnp.abs(s - target)
-        spread = 3.0 * (q - p) + jnp.abs(r - s)
+        outer = jnp.maximum(high_ab, high_cd) - jnp.minimum(low_ab, low_cd)
+        inner = jnp.abs(jnp.minimum(high_ab, high_cd) - jnp.maximum(low_ab, low_cd))
+        spread = 3.0 * outer + inner
         group = (first + i >= ATMOS).astype(jnp.int32)
         value = (skill * (1.0 / MEMBERS) - (2.0 * COEFF) * spread) * weight[group]
         values[i] = value

time: 81.7 us -> 81.7 us (level)
  no operation moved by 1% of the time
where the time goes in v8:
time: 81.7 us; the launch traced here: 81.3 us
  waiting for transfers between devices  31 us (38%)
  starting transfers between devices  28 us (34%)
  blocking collectives  16.5 us (20%)
  Pallas kernels  4.94 us (6%)
    all_to_all x1, waiting for transfers between devices, shards(): lax.all_to_all(ensemble_prediction[0], 'member', split_axis=0, concat_axi...  27.9 us
    all_to_all x1, blocking collectives, exchanged(): return lax.all_to_all(copies, axes, split_axis=0, concat_axis=0, tiled=True)  16.5 us
    all_to_all x1, starting transfers between devices, exchanged(): return lax.all_to_all(copies, axes, split_axis=0, concat_axis=0, tiled=True)  14 us
    all_to_all x1, starting transfers between devices, shards(): lax.all_to_all(ensemble_prediction[0], 'member', split_axis=0, concat_axi...  5.56 us
    ppermute x1, starting transfers between devices, add_up_and_send(): beside = lax.ppermute(codes, 'member', BESIDE)  3.78 us
    all_to_all x1, waiting for transfers between devices, exchanged(): return lax.all_to_all(copies, axes, split_axis=0, concat_axis=0, tiled=True)  3.14 us
    pallas_call x1, Pallas kernels, decode(): pl.pallas_call(decode_kernel, out_shape=(jax.ShapeDtypeStruct((VARIABLE_N...  3.01 us
    ppermute x1, starting transfers between devices, add_up_and_send(): corner = lax.ppermute(codes, 'member', CORNER)  2.68 us
  transfers between devices with their start and end apart: 5, of which 2 were waited for; matrix products, arithmetic and copies ran while one was open for 0% of the time, Pallas kernels for 0%

profile of v8, /device:TPU:1, one launch (start us, length us, event | category | flops | bytes accessed | tf_op | source)
XLA Modules:
  0.0 81.3 jit_solution(4211795217134633101)
XLA Ops:
  0.6 0.0 copy-start.1
  0.6 0.0 copy-start
  0.6 5.6 %all-to-all-start.2 = ((bf16[300,16,128]{2,1,0:T(8,128)(2,1)}), bf16[300,16,128]{2,1,0:T(8,128)(2,1)S(1)}, u32[]{:S(2)}, u32[]{:S(2)}) async-start(bf16[300,16,128]{2,1,0:T(8,128)(2,1)} %bitcast.4), calls=%async_computation.2 | async-start | bytes 2457600 | tf_op jit(solution)/shard_map/all_to_all | solution.py:203
  6.2 0.1 fusion.6
  6.3 0.0 copy-done.1
  6.3 27.9 %all-to-all-done.2 = bf16[300,16,128]{2,1,0:T(8,128)(2,1)S(1)} async-done(((bf16[300,16,128]{2,1,0:T(8,128)(2,1)}), bf16[300,16,128]{2,1,0:T(8,128)(2,1)S(1)}, u32[]{:S(2)}, u32[]{:S(2)}) %all-to-all-start.2) | async-done | bytes 1228832 | tf_op jit(solution)/shard_map/all_to_all | solution.py:203
  34.2 0.0 copy-done
  34.2 1.9 %shard_map.50 = (s32[38,16,128]{2,1,0:T(8,128)S(1)}, f32[320,1,128]{2,1,0:T(1,128)}) custom-call(s32[1]{0:T(128)} %bitcast.member, bf16[4,75,16,128]{3,2,1,0:T(8,128)(2,1)S(1)} %bitcast.3, bf16[300,16,128]{2,1,0:T(8,128)(2,1)S(1)} %copy-done, f32[2,16,128]{2,1,0:T(8,128)S(1)} %compare_select_fusion.weight), custom_call_target="tpu_custom_call" | custom-call | flops 4608000 | bytes 2150400 | tf_op jit(solution)/shard_map/pallas_call | solution.py:84
  36.1 1.9 %collective-permute-start.2 = (s32[38,16,128]{2,1,0:T(8,128)S(1)}, s32[38,16,128]{2,1,0:T(8,128)S(1)}, u32[]{:S(2)}, u32[]{:S(2)}) collective-permute-start(s32[38,16,128]{2,1,0:T(8,128)S(1)} %get-tuple-element.24.own), channel_id=1, source_target_pairs={{0,256},{128,384},{256,0},{384,128},{1,257},{129,385},{257,1},{385... | collective-permute-start | bytes 933896 | tf_op jit(solution)/shard_map/ppermute | solution.py:220
  38.0 40.2 %conditional.2 = (s32[38,16,128]{2,1,0:T(8,128)}, s32[38,16,128]{2,1,0:T(8,128)}, f32[16,1,128]{2,1,0:T(1,128)}) conditional(s32[]{:T(128)} %convert_element_type.15, () %tuple.22, (s32[38,16,128]{2,1,0:T(8,128)S(1)}, pred[]{:T(512)}, f32[320,1,128]{2,1,0:T(1,128)}) %tuple.23), branch_computations={%region_0.1_spmd, %region_1.5_spmd} | conditional | flops 3969 | bytes 3024021 | solution.py:198
  38.0 14.0 %all-to-all-start.1 = ((f32[320,1,128]{2,1,0:T(1,128)}), f32[320,1,128]{2,1,0:T(1,128)S(1)}, u32[]{:S(2)}, u32[]{:S(2)}) async-start(f32[320,1,128]{2,1,0:T(1,128)} %get-tuple-element.16), calls=%async_computation.1 | async-start | bytes 327680 | tf_op jit(solution)/shard_map/cond/branch_1_fun/all_to_all | solution.py:193
  52.1 2.7 %collective-permute-start.1 = (s32[38,16,128]{2,1,0:T(8,128)S(1)}, s32[38,16,128]{2,1,0:T(8,128)}, u32[]{:S(2)}, u32[]{:S(2)}) collective-permute-start(s32[38,16,128]{2,1,0:T(8,128)S(1)} %get-tuple-element.14), channel_id=1, source_target_pairs={{0,384},{128,256},{256,128},{384,0},{1,385},{129,257},{257,129},{3... | collective-permute-start | bytes 933896 | tf_op jit(solution)/shard_map/cond/branch_1_fun/ppermute | solution.py:224
  54.8 3.8 %collective-permute-start = (s32[38,16,128]{2,1,0:T(8,128)S(1)}, s32[38,16,128]{2,1,0:T(8,128)}, u32[]{:S(2)}, u32[]{:S(2)}) collective-permute-start(s32[38,16,128]{2,1,0:T(8,128)S(1)} %get-tuple-element.14), channel_id=1, source_target_pairs={{0,128},{128,0},{256,384},{384,256},{1,129},{129,1},{257,385},{385... | collective-permute-start | bytes 933896 | tf_op jit(solution)/shard_map/cond/branch_1_fun/ppermute | solution.py:223
  58.6 3.1 %all-to-all-done.1 = f32[320,1,128]{2,1,0:T(1,128)S(1)} async-done(((f32[320,1,128]{2,1,0:T(1,128)}), f32[320,1,128]{2,1,0:T(1,128)S(1)}, u32[]{:S(2)}, u32[]{:S(2)}) %all-to-all-start.1) | async-done | bytes 163872 | tf_op jit(solution)/shard_map/cond/branch_1_fun/all_to_all | solution.py:193
  61.7 16.6 %conditional = (f32[16,1,128]{2,1,0:T(1,128)}) conditional(s32[]{:T(128)} %convert_element_type.12, () %tuple.17, f32[320,1,128]{2,1,0:T(1,128)S(1)} %all-to-all-done.1), branch_computations={%region_2.2_spmd, %region_3.4_spmd} | conditional | flops 3968 | bytes 41992 | solution.py:198
  61.8 16.5 %all_to_all.14 = f32[16,1,128]{2,1,0:T(1,128)} all-to-all(f32[16,1,128]{2,1,0:T(1,128)S(1)} %broadcast_in_dim.4), channel_id=1, replica_groups=mesh['member'=4,'space_0'=8,'space_1'=2,'space_2'=4,'space_3'=2] {'membe..., dimensions={0} | all-to-all | bytes 16384 | tf_op jit(solution)/shard_map/cond/branch_1_fun/cond/branch_1_fun/all_to_all | solution.py:193
  78.3 0.0 collective-permute-done.1
  78.3 0.0 collective-permute-done
  78.3 0.0 collective-permute-done.2.across
  78.3 3.0 %shard_map.51 = (f32[300,16,128]{2,1,0:T(8,128)}, f32[300]{0:T(512)}) custom-call(s32[1]{0:T(128)} %bitcast.member, f32[16,1,128]{2,1,0:T(1,128)} %get-tuple-element.26.sums_here, s32[38,16,128]{2,1,0:T(8,128)S(1)} %get-tuple-element.24.own, s32[38,16,128]{2,1,0:T(8,128)S(1)} %collective-permute-done.2.across, s32[38,16,128]{2,1,0:T(8,128)} %get-tuple-element.27.beside, ...), custom_call_target="tpu_custom_call" | custom-call | flops 4980736 | bytes 3735552 | tf_op jit(solution)/shard_map/pallas_call | solution.py:166
  (3 shorter events, 0.1 us)
Async XLA Ops:
  0.6 5.7 %copy-start.1 = (s32[2,16,128]{2,1,0:T(8,128)S(1)}, s32[2,16,128]{2,1,0:T(8,128)}, u32[]{:S(2)}) copy-start(s32[2,16,128]{2,1,0:T(8,128)} %param.9) | copy-start | bytes 49156
  0.6 33.5 %copy-start = (bf16[300,16,128]{2,1,0:T(8,128)(2,1)S(1)}, bf16[300,16,128]{2,1,0:T(8,128)(2,1)}, u32[]{:S(2)}) copy-start(bf16[300,16,128]{2,1,0:T(8,128)(2,1)} %obs.1) | copy-start | bytes 3686404
  0.6 33.5 %all-to-all-start.2 = ((bf16[300,16,128]{2,1,0:T(8,128)(2,1)}), bf16[300,16,128]{2,1,0:T(8,128)(2,1)S(1)}, u32[]{:S(2)}, u32[]{:S(2)}) async-start(bf16[300,16,128]{2,1,0:T(8,128)(2,1)} %bitcast.4), calls=%async_computation.2 | async-start | bytes 2457600 | tf_op jit(solution)/shard_map/all_to_all | solution.py:203
  36.1 42.2 %collective-permute-start.2 = (s32[38,16,128]{2,1,0:T(8,128)S(1)}, s32[38,16,128]{2,1,0:T(8,128)S(1)}, u32[]{:S(2)}, u32[]{:S(2)}) collective-permute-start(s32[38,16,128]{2,1,0:T(8,128)S(1)} %get-tuple-element.24.own), channel_id=1, source_target_pairs={{0,256},{128,384},{256,0},{384,128},{1,257},{129,385},{257,1},{385... | collective-permute-start | bytes 933896 | tf_op jit(solution)/shard_map/ppermute | solution.py:220
  38.0 23.7 %all-to-all-start.1 = ((f32[320,1,128]{2,1,0:T(1,128)}), f32[320,1,128]{2,1,0:T(1,128)S(1)}, u32[]{:S(2)}, u32[]{:S(2)}) async-start(f32[320,1,128]{2,1,0:T(1,128)} %get-tuple-element.16), calls=%async_computation.1 | async-start | bytes 327680 | tf_op jit(solution)/shard_map/cond/branch_1_fun/all_to_all | solution.py:193
  52.1 26.2 %collective-permute-start.1 = (s32[38,16,128]{2,1,0:T(8,128)S(1)}, s32[38,16,128]{2,1,0:T(8,128)}, u32[]{:S(2)}, u32[]{:S(2)}) collective-permute-start(s32[38,16,128]{2,1,0:T(8,128)S(1)} %get-tuple-element.14), channel_id=1, source_target_pairs={{0,384},{128,256},{256,128},{384,0},{1,385},{129,257},{257,129},{3... | collective-permute-start | bytes 933896 | tf_op jit(solution)/shard_map/cond/branch_1_fun/ppermute | solution.py:224
  54.8 23.5 %collective-permute-start = (s32[38,16,128]{2,1,0:T(8,128)S(1)}, s32[38,16,128]{2,1,0:T(8,128)}, u32[]{:S(2)}, u32[]{:S(2)}) collective-permute-start(s32[38,16,128]{2,1,0:T(8,128)S(1)} %get-tuple-element.14), channel_id=1, source_target_pairs={{0,128},{128,0},{256,384},{384,256},{1,129},{129,1},{257,385},{385... | collective-permute-start | bytes 933896 | tf_op jit(solution)/shard_map/cond/branch_1_fun/ppermute | solution.py:223

commit v9 on v8

--- a/solution.py
+++ b/solution.py
@@ -45,7 +45,7 @@
         return jnp.maximum(top, jnp.abs(value))
 
     rows[...] = jnp.zeros(rows.shape, jnp.float32)
-    top = lax.fori_loop(0, SHARE, score, jnp.zeros(values.shape[1:], jnp.float32), unroll=5)
+    top = lax.fori_loop(0, SHARE, score, jnp.zeros(values.shape[1:], jnp.float32), unroll=3)
     for g in range(2):
         rows[SHARE + g : SHARE + g + 1, :] = jnp.sum(weight[g], axis=0, keepdims=True)
         valid = (weight[g] > 0.0).astype(jnp.float32)

time: 81.7 us -> 81.8 us (level)
  no operation moved by 1% of the time
where the time goes in v9:
time: 81.8 us; the launch traced here: 81.4 us
  waiting for transfers between devices  31 us (38%)
  starting transfers between devices  28 us (34%)
  blocking collectives  16.5 us (20%)
  Pallas kernels  5.05 us (6%)
    all_to_all x1, waiting for transfers between devices, shards(): lax.all_to_all(ensemble_prediction[0], 'member', split_axis=0, concat_axi...  27.9 us
    all_to_all x1, blocking collectives, exchanged(): return lax.all_to_all(copies, axes, split_axis=0, concat_axis=0, tiled=True)  16.5 us
    all_to_all x1, starting transfers between devices, exchanged(): return lax.all_to_all(copies, axes, split_axis=0, concat_axis=0, tiled=True)  14 us
    all_to_all x1, starting transfers between devices, shards(): lax.all_to_all(ensemble_prediction[0], 'member', split_axis=0, concat_axi...  5.56 us
    ppermute x1, starting transfers between devices, add_up_and_send(): beside = lax.ppermute(codes, 'member', BESIDE)  3.77 us
    all_to_all x1, waiting for transfers between devices, exchanged(): return lax.all_to_all(copies, axes, split_axis=0, concat_axis=0, tiled=True)  3.14 us
    pallas_call x1, Pallas kernels, decode(): pl.pallas_call(decode_kernel, out_shape=(jax.ShapeDtypeStruct((VARIABLE_N...  3.01 us
    ppermute x1, starting transfers between devices, add_up_and_send(): corner = lax.ppermute(codes, 'member', CORNER)  2.68 us
  transfers between devices with their start and end apart: 5, of which 2 were waited for; matrix products, arithmetic and copies ran while one was open for 0% of the time, Pallas kernels for 0%

profile of v9, /device:TPU:1, one launch (start us, length us, event | category | flops | bytes accessed | tf_op | source)
XLA Modules:
  0.0 81.4 jit_solution(16124750542308484451)
XLA Ops:
  0.6 0.0 copy-start.1
  0.6 0.0 copy-start
  0.6 5.6 %all-to-all-start.2 = ((bf16[300,16,128]{2,1,0:T(8,128)(2,1)}), bf16[300,16,128]{2,1,0:T(8,128)(2,1)S(1)}, u32[]{:S(2)}, u32[]{:S(2)}) async-start(bf16[300,16,128]{2,1,0:T(8,128)(2,1)} %bitcast.4), calls=%async_computation.2 | async-start | bytes 2457600 | tf_op jit(solution)/shard_map/all_to_all | solution.py:203
  6.2 0.1 fusion.6
  6.3 0.0 copy-done.1
  6.3 27.9 %all-to-all-done.2 = bf16[300,16,128]{2,1,0:T(8,128)(2,1)S(1)} async-done(((bf16[300,16,128]{2,1,0:T(8,128)(2,1)}), bf16[300,16,128]{2,1,0:T(8,128)(2,1)S(1)}, u32[]{:S(2)}, u32[]{:S(2)}) %all-to-all-start.2) | async-done | bytes 1228832 | tf_op jit(solution)/shard_map/all_to_all | solution.py:203
  34.2 0.0 copy-done
  34.2 2.0 %shard_map.50 = (s32[38,16,128]{2,1,0:T(8,128)S(1)}, f32[320,1,128]{2,1,0:T(1,128)}) custom-call(s32[1]{0:T(128)} %bitcast.member, bf16[4,75,16,128]{3,2,1,0:T(8,128)(2,1)S(1)} %bitcast.3, bf16[300,16,128]{2,1,0:T(8,128)(2,1)S(1)} %copy-done, f32[2,16,128]{2,1,0:T(8,128)S(1)} %compare_select_fusion.weight), custom_call_target="tpu_custom_call" | custom-call | flops 4608000 | bytes 2150400 | tf_op jit(solution)/shard_map/pallas_call | solution.py:84
  36.2 1.9 %collective-permute-start.2 = (s32[38,16,128]{2,1,0:T(8,128)S(1)}, s32[38,16,128]{2,1,0:T(8,128)S(1)}, u32[]{:S(2)}, u32[]{:S(2)}) collective-permute-start(s32[38,16,128]{2,1,0:T(8,128)S(1)} %get-tuple-element.24.own), channel_id=1, source_target_pairs={{0,256},{128,384},{256,0},{384,128},{1,257},{129,385},{257,1},{385... | collective-permute-start | bytes 933896 | tf_op jit(solution)/shard_map/ppermute | solution.py:220
  38.1 40.3 %conditional.2 = (s32[38,16,128]{2,1,0:T(8,128)}, s32[38,16,128]{2,1,0:T(8,128)}, f32[16,1,128]{2,1,0:T(1,128)}) conditional(s32[]{:T(128)} %convert_element_type.15, () %tuple.22, (s32[38,16,128]{2,1,0:T(8,128)S(1)}, pred[]{:T(512)}, f32[320,1,128]{2,1,0:T(1,128)}) %tuple.23), branch_computations={%region_0.1_spmd, %region_1.5_spmd} | conditional | flops 3969 | bytes 3024021 | solution.py:198
  38.2 14.0 %all-to-all-start.1 = ((f32[320,1,128]{2,1,0:T(1,128)}), f32[320,1,128]{2,1,0:T(1,128)S(1)}, u32[]{:S(2)}, u32[]{:S(2)}) async-start(f32[320,1,128]{2,1,0:T(1,128)} %get-tuple-element.16), calls=%async_computation.1 | async-start | bytes 327680 | tf_op jit(solution)/shard_map/cond/branch_1_fun/all_to_all | solution.py:193
  52.2 2.7 %collective-permute-start.1 = (s32[38,16,128]{2,1,0:T(8,128)S(1)}, s32[38,16,128]{2,1,0:T(8,128)}, u32[]{:S(2)}, u32[]{:S(2)}) collective-permute-start(s32[38,16,128]{2,1,0:T(8,128)S(1)} %get-tuple-element.14), channel_id=1, source_target_pairs={{0,384},{128,256},{256,128},{384,0},{1,385},{129,257},{257,129},{3... | collective-permute-start | bytes 933896 | tf_op jit(solution)/shard_map/cond/branch_1_fun/ppermute | solution.py:224
  54.9 3.8 %collective-permute-start = (s32[38,16,128]{2,1,0:T(8,128)S(1)}, s32[38,16,128]{2,1,0:T(8,128)}, u32[]{:S(2)}, u32[]{:S(2)}) collective-permute-start(s32[38,16,128]{2,1,0:T(8,128)S(1)} %get-tuple-element.14), channel_id=1, source_target_pairs={{0,128},{128,0},{256,384},{384,256},{1,129},{129,1},{257,385},{385... | collective-permute-start | bytes 933896 | tf_op jit(solution)/shard_map/cond/branch_1_fun/ppermute | solution.py:223
  58.7 3.1 %all-to-all-done.1 = f32[320,1,128]{2,1,0:T(1,128)S(1)} async-done(((f32[320,1,128]{2,1,0:T(1,128)}), f32[320,1,128]{2,1,0:T(1,128)S(1)}, u32[]{:S(2)}, u32[]{:S(2)}) %all-to-all-start.1) | async-done | bytes 163872 | tf_op jit(solution)/shard_map/cond/branch_1_fun/all_to_all | solution.py:193
  61.8 16.6 %conditional = (f32[16,1,128]{2,1,0:T(1,128)}) conditional(s32[]{:T(128)} %convert_element_type.12, () %tuple.17, f32[320,1,128]{2,1,0:T(1,128)S(1)} %all-to-all-done.1), branch_computations={%region_2.2_spmd, %region_3.4_spmd} | conditional | flops 3968 | bytes 41992 | solution.py:198
  61.9 16.5 %all_to_all.14 = f32[16,1,128]{2,1,0:T(1,128)} all-to-all(f32[16,1,128]{2,1,0:T(1,128)S(1)} %broadcast_in_dim.4), channel_id=1, replica_groups=mesh['member'=4,'space_0'=8,'space_1'=2,'space_2'=4,'space_3'=2] {'membe..., dimensions={0} | all-to-all | bytes 16384 | tf_op jit(solution)/shard_map/cond/branch_1_fun/cond/branch_1_fun/all_to_all | solution.py:193
  78.4 0.0 collective-permute-done.1
  78.4 0.0 collective-permute-done
  78.4 0.0 collective-permute-done.2.across
  78.4 3.0 %shard_map.51 = (f32[300,16,128]{2,1,0:T(8,128)}, f32[300]{0:T(512)}) custom-call(s32[1]{0:T(128)} %bitcast.member, f32[16,1,128]{2,1,0:T(1,128)} %get-tuple-element.26.sums_here, s32[38,16,128]{2,1,0:T(8,128)S(1)} %get-tuple-element.24.own, s32[38,16,128]{2,1,0:T(8,128)S(1)} %collective-permute-done.2.across, s32[38,16,128]{2,1,0:T(8,128)} %get-tuple-element.27.beside, ...), custom_call_target="tpu_custom_call" | custom-call | flops 4980736 | bytes 3735552 | tf_op jit(solution)/shard_map/pallas_call | solution.py:166
  (3 shorter events, 0.1 us)
Async XLA Ops:
  0.6 5.7 %copy-start.1 = (s32[2,16,128]{2,1,0:T(8,128)S(1)}, s32[2,16,128]{2,1,0:T(8,128)}, u32[]{:S(2)}) copy-start(s32[2,16,128]{2,1,0:T(8,128)} %param.9) | copy-start | bytes 49156
  0.6 33.5 %copy-start = (bf16[300,16,128]{2,1,0:T(8,128)(2,1)S(1)}, bf16[300,16,128]{2,1,0:T(8,128)(2,1)}, u32[]{:S(2)}) copy-start(bf16[300,16,128]{2,1,0:T(8,128)(2,1)} %obs.1) | copy-start | bytes 3686404
  0.6 33.5 %all-to-all-start.2 = ((bf16[300,16,128]{2,1,0:T(8,128)(2,1)}), bf16[300,16,128]{2,1,0:T(8,128)(2,1)S(1)}, u32[]{:S(2)}, u32[]{:S(2)}) async-start(bf16[300,16,128]{2,1,0:T(8,128)(2,1)} %bitcast.4), calls=%async_computation.2 | async-start | bytes 2457600 | tf_op jit(solution)/shard_map/all_to_all | solution.py:203
  36.2 42.2 %collective-permute-start.2 = (s32[38,16,128]{2,1,0:T(8,128)S(1)}, s32[38,16,128]{2,1,0:T(8,128)S(1)}, u32[]{:S(2)}, u32[]{:S(2)}) collective-permute-start(s32[38,16,128]{2,1,0:T(8,128)S(1)} %get-tuple-element.24.own), channel_id=1, source_target_pairs={{0,256},{128,384},{256,0},{384,128},{1,257},{129,385},{257,1},{385... | collective-permute-start | bytes 933896 | tf_op jit(solution)/shard_map/ppermute | solution.py:220
  38.2 23.7 %all-to-all-start.1 = ((f32[320,1,128]{2,1,0:T(1,128)}), f32[320,1,128]{2,1,0:T(1,128)S(1)}, u32[]{:S(2)}, u32[]{:S(2)}) async-start(f32[320,1,128]{2,1,0:T(1,128)} %get-tuple-element.16), calls=%async_computation.1 | async-start | bytes 327680 | tf_op jit(solution)/shard_map/cond/branch_1_fun/all_to_all | solution.py:193
  52.2 26.2 %collective-permute-start.1 = (s32[38,16,128]{2,1,0:T(8,128)S(1)}, s32[38,16,128]{2,1,0:T(8,128)}, u32[]{:S(2)}, u32[]{:S(2)}) collective-permute-start(s32[38,16,128]{2,1,0:T(8,128)S(1)} %get-tuple-element.14), channel_id=1, source_target_pairs={{0,384},{128,256},{256,128},{384,0},{1,385},{129,257},{257,129},{3... | collective-permute-start | bytes 933896 | tf_op jit(solution)/shard_map/cond/branch_1_fun/ppermute | solution.py:224
  54.9 23.5 %collective-permute-start = (s32[38,16,128]{2,1,0:T(8,128)S(1)}, s32[38,16,128]{2,1,0:T(8,128)}, u32[]{:S(2)}, u32[]{:S(2)}) collective-permute-start(s32[38,16,128]{2,1,0:T(8,128)S(1)} %get-tuple-element.14), channel_id=1, source_target_pairs={{0,128},{128,0},{256,384},{384,256},{1,129},{129,1},{257,385},{385... | collective-permute-start | bytes 933896 | tf_op jit(solution)/shard_map/cond/branch_1_fun/ppermute | solution.py:223
